TPU v7x, 256 devices: a whole 4x4x8 slice. The times are simulated.
256 devices in a mesh: seq: 64 (over z, y, core), head: 4 (over x).
Axes of the slice: x: 4, y: 4, z: 8, core: 2. Of those that a mesh axis runs over, the one named last changes fastest.
Arguments:
- video_q: bfloat16 [16384, 3072], P('seq', 'head'), may hold values from -200 to 200
- video_k: bfloat16 [16384, 3072], P('seq', 'head'), may hold values from -200 to 200
- video_v: bfloat16 [16384, 3072], P('seq', 'head'), may hold values from -6 to 6
- audio_q: bfloat16 [16384, 3072], P('seq', 'head'), may hold values from -200 to 200
- audio_k: bfloat16 [16384, 3072], P('seq', 'head'), may hold values from -200 to 200
- audio_v: bfloat16 [16384, 3072], P('seq', 'head'), may hold values from -6 to 6
- video_q_gain: float32 [3072], P('head'), may hold values from 0.1 to 1.9
- audio_k_gain: float32 [3072], P('head'), may hold values from 0.1 to 1.9
- audio_q_gain: float32 [3072], P('head'), may hold values from 0.1 to 1.9
- video_k_gain: float32 [3072], P('head'), may hold values from 0.1 to 1.9
- tile_first: int32 [64], replicated, may hold values from 0 to 63, as said below
- tile_count: int32 [64], replicated, may hold values from 1 to 5
Outputs:
- video_out: bfloat16 [16384, 3072], P('seq', 'head')
- audio_out: bfloat16 [16384, 3072], P('seq', 'head')
Inputs may be any that keep to these rules, and one draw needn't show every extreme that they name: Stretch c intersects tiles tile_first[c] .. tile_first[c] + tile_count[c] - 1, which include tile c and lie within c - 2 .. c + 2.
All inputs are finite; a program needn't handle non-finite values.
Results may differ from a plain program's by a relative error of at most 0.017.
Values may be sent and summed in bfloat16 or wider, within the bound.
A program may use at most 64 MiB of HBM per device.

v0:
```python
import jax
import jax.numpy as jnp
from jax import lax
from jax.sharding import PartitionSpec as P

HEAD_DIM = 128
REACH = 2


EPS = 1e-06
NEG = -1e30


def shifted(array, axis, by):
    length = lax.axis_size(axis)
    pairs = [(i, i + by) for i in range(length) if 0 <= i + by < length]
    return lax.ppermute(array, axis, pairs)


def squares(x):
    wide = x.astype(jnp.float32)
    return jnp.sum(wide * wide, axis=1)


def normalize(x, total, width, gain):
    scale = lax.rsqrt(total / width + EPS)
    return (x.astype(jnp.float32) * scale[:, None] * gain).astype(jnp.bfloat16)


def covers(stretch, tile, tile_first, tile_count, count_all):
    safe = jnp.clip(stretch, 0, count_all - 1)
    first = lax.dynamic_index_in_dim(tile_first, safe, keepdims=False)
    count = lax.dynamic_index_in_dim(tile_count, safe, keepdims=False)
    inside = (stretch >= 0) & (stretch < count_all) & (tile >= 0) & (tile < count_all)
    return inside & (tile >= first) & (tile < first + count)


def partial_attend(query, keys, values, valid):
    rows = query.shape[0]
    length = keys.shape[0]
    heads = query.shape[1] // HEAD_DIM
    qh = query.reshape(rows, heads, HEAD_DIM)
    kh = keys.reshape(length, heads, HEAD_DIM)
    vh = values.reshape(length, heads, HEAD_DIM)
    scores = jnp.einsum("qhe,khe->hqk", qh, kh, preferred_element_type=jnp.float32) * HEAD_DIM ** (
        -0.5
    )
    scores = jnp.where(valid, scores, NEG)
    top = jnp.max(scores, axis=2)
    weights = jnp.where(valid, jnp.exp(scores - top[:, :, None]), 0.0)
    total = jnp.sum(weights, axis=2)
    mixed = jnp.einsum(
        "hqk,khe->qhe", weights.astype(jnp.bfloat16), vh, preferred_element_type=jnp.float32
    )
    return (top, total, mixed)


def combine(state, other):
    top_a, total_a, mixed_a = state
    top_b, total_b, mixed_b = other
    top = jnp.maximum(top_a, top_b)
    factor_a = jnp.exp(top_a - top)
    factor_b = jnp.exp(top_b - top)
    total = total_a * factor_a + total_b * factor_b
    mixed = (
        mixed_a * jnp.transpose(factor_a)[:, :, None]
        + mixed_b * jnp.transpose(factor_b)[:, :, None]
    )
    return (top, total, mixed)


def finish(state):
    top, total, mixed = state
    rows = mixed.shape[0]
    result = mixed / jnp.transpose(total)[:, :, None]
    return result.reshape(rows, mixed.shape[1] * HEAD_DIM).astype(jnp.bfloat16)


def local(
    video_q,
    video_k,
    video_v,
    audio_q,
    audio_k,
    audio_v,
    video_q_gain,
    audio_k_gain,
    audio_q_gain,
    video_k_gain,
    tile_first,
    tile_count,
):
    width = video_q.shape[1] * lax.axis_size("head")
    sums = lax.psum(
        (squares(video_q), squares(audio_k), squares(audio_q), squares(video_k)), "head"
    )
    nvq = normalize(video_q, sums[0], width, video_q_gain)
    nak = normalize(audio_k, sums[1], width, audio_k_gain)
    naq = normalize(audio_q, sums[2], width, audio_q_gain)
    nvk = normalize(video_k, sums[3], width, video_k_gain)
    count_all = lax.axis_size("seq")
    me = lax.axis_index("seq")
    video_state = partial_attend(
        nvq, nak, audio_v, covers(me, me, tile_first, tile_count, count_all)
    )
    audio_state = partial_attend(
        naq, nvk, video_v, covers(me, me, tile_first, tile_count, count_all)
    )
    distances = [dist for dist in range(-REACH, REACH + 1) if dist != 0]
    for dist in distances:
        source = me - dist
        far_vk, far_vv, far_ak, far_av = shifted((nvk, video_v, nak, audio_v), "seq", dist)
        video_state = combine(
            video_state,
            partial_attend(
                nvq, far_ak, far_av, covers(source, me, tile_first, tile_count, count_all)
            ),
        )
        audio_state = combine(
            audio_state,
            partial_attend(
                naq, far_vk, far_vv, covers(me, source, tile_first, tile_count, count_all)
            ),
        )
    return (finish(video_state), finish(audio_state))


def solution(mesh):
    return jax.shard_map(
        local,
        mesh=mesh,
        in_specs=(
            P("seq", "head"),
            P("seq", "head"),
            P("seq", "head"),
            P("seq", "head"),
            P("seq", "head"),
            P("seq", "head"),
            P("head"),
            P("head"),
            P("head"),
            P("head"),
            P(),
            P(),
        ),
        out_specs=(P("seq", "head"), P("seq", "head")),
        check_vma=False,
    )
```

profile of v0, /device:TPU:136, one launch (start us, length us, event | category | flops | bytes accessed | tf_op | source)
XLA Modules:
  0.0 160.1 jit_solution(867229492834137129)
XLA Ops:
  4.0 10.5 %all-reduce = (f32[256]{0:T(256)S(1)}, f32[256]{0:T(256)S(1)}, f32[256]{0:T(256)S(1)}, f32[256]{0:T(256)S(1)}) all-reduce(f32[256]{0:T(256)S(1)} %fusion.48, f32[256]{0:T(256)S(1)} %fusion.51, f32[256]{0:T(256)S(1)} %fusion.54, f32[256]{0:T(256)S(1)} %fusion.57), channel_id=1, replica_groups=mesh['seq'=64,'head'=4] {'head'}, use_global_device_ids=true, to_apply=%region_1.0 | all-reduce | flops 1024 | bytes 8192 | tf_op jit(solution)/shard_map/psum | solution.py:94
  15.4 3.5 %collective-permute-start.6 = (bf16[256,768]{0,1:T(8,128)(2,1)}, bf16[256,768]{0,1:T(8,128)(2,1)}, u32[]{:S(2)}, u32[]{:S(2)}) collective-permute-start(bf16[256,768]{0,1:T(8,128)(2,1)} %fusion.53), channel_id=1, source_target_pairs={{0,8},{4,12},{8,16},{12,20},{16,24},{20,28},{24,32},{28,36},{32,40... | collective-permute-start | bytes 1179656 | tf_op jit(solution)/shard_map/ppermute | solution.py:17
  18.9 1.9 %collective-permute-start.4 = (bf16[256,768]{0,1:T(8,128)(2,1)}, bf16[256,768]{0,1:T(8,128)(2,1)}, u32[]{:S(2)}, u32[]{:S(2)}) collective-permute-start(bf16[256,768]{0,1:T(8,128)(2,1)} %fusion.53), channel_id=1, source_target_pairs={{0,4},{4,8},{8,12},{12,16},{16,20},{20,24},{24,28},{28,32},{32,36}... | collective-permute-start | bytes 1179656 | tf_op jit(solution)/shard_map/ppermute | solution.py:17
  20.8 3.6 %collective-permute-start.2 = (bf16[256,768]{0,1:T(8,128)(2,1)}, bf16[256,768]{0,1:T(8,128)(2,1)}, u32[]{:S(2)}, u32[]{:S(2)}) collective-permute-start(bf16[256,768]{0,1:T(8,128)(2,1)} %fusion.53), channel_id=1, source_target_pairs={{4,0},{8,4},{12,8},{16,12},{20,16},{24,20},{28,24},{32,28},{36,32}... | collective-permute-start | bytes 1179656 | tf_op jit(solution)/shard_map/ppermute | solution.py:17
  24.5 5.7 %collective-permute-start = (bf16[256,768]{0,1:T(8,128)(2,1)}, bf16[256,768]{0,1:T(8,128)(2,1)}, u32[]{:S(2)}, u32[]{:S(2)}) collective-permute-start(bf16[256,768]{0,1:T(8,128)(2,1)} %fusion.53), channel_id=1, source_target_pairs={{8,0},{12,4},{16,8},{20,12},{24,16},{28,20},{32,24},{36,28},{40,32... | collective-permute-start | bytes 1179656 | tf_op jit(solution)/shard_map/ppermute | solution.py:17
  30.2 1.9 %collective-permute-start.7 = (bf16[256,768]{1,0:T(8,128)(2,1)}, bf16[256,768]{1,0:T(8,128)(2,1)}, u32[]{:S(2)}, u32[]{:S(2)}) collective-permute-start(bf16[256,768]{1,0:T(8,128)(2,1)} %param.17), channel_id=1, source_target_pairs={{0,8},{4,12},{8,16},{12,20},{16,24},{20,28},{24,32},{28,36},{32,40... | collective-permute-start | bytes 1179656 | tf_op jit(solution)/shard_map/ppermute | solution.py:17
  32.1 1.9 %copy.52 = bf16[256,768]{0,1:T(8,128)(2,1)} copy(bf16[256,768]{1,0:T(8,128)(2,1)} %param.17) | data formatting | bytes 786432 | tf_op args[5]
  46.4 1.9 %copy.74 = bf16[256,768]{0,1:T(8,128)(2,1)} copy(bf16[256,768]{1,0:T(8,128)(2,1)} %param.14) | data formatting | bytes 786432 | tf_op args[2]
  57.4 3.6 %collective-permute-start.3 = (bf16[256,768]{1,0:T(8,128)(2,1)}, bf16[256,768]{1,0:T(8,128)(2,1)}, u32[]{:S(2)}, u32[]{:S(2)}) collective-permute-start(bf16[256,768]{1,0:T(8,128)(2,1)} %param.17), channel_id=1, source_target_pairs={{4,0},{8,4},{12,8},{16,12},{20,16},{24,20},{28,24},{32,28},{36,32}... | collective-permute-start | bytes 1179656 | tf_op jit(solution)/shard_map/ppermute | solution.py:17
  62.6 7.2 %collective-permute-start.1 = (bf16[256,768]{1,0:T(8,128)(2,1)}, bf16[256,768]{1,0:T(8,128)(2,1)}, u32[]{:S(2)}, u32[]{:S(2)}) collective-permute-start(bf16[256,768]{1,0:T(8,128)(2,1)} %param.17), channel_id=1, source_target_pairs={{8,0},{12,4},{16,8},{20,12},{24,16},{28,20},{32,24},{36,28},{40,32... | collective-permute-start | bytes 1179656 | tf_op jit(solution)/shard_map/ppermute | solution.py:17
  77.9 1.9 %collective-permute-start.15 = (bf16[256,768]{1,0:T(8,128)(2,1)}, bf16[256,768]{1,0:T(8,128)(2,1)}, u32[]{:S(2)}, u32[]{:S(2)}) collective-permute-start(bf16[256,768]{1,0:T(8,128)(2,1)} %param.14), channel_id=1, source_target_pairs={{0,8},{4,12},{8,16},{12,20},{16,24},{20,28},{24,32},{28,36},{32,40... | collective-permute-start | bytes 1179656 | tf_op jit(solution)/shard_map/ppermute | solution.py:17
  79.8 1.9 %copy.68 = bf16[256,768]{0,1:T(8,128)(2,1)} copy(bf16[256,768]{1,0:T(8,128)(2,1)} %collective-permute-done.7) | data formatting | bytes 786432 | tf_op jit(solution)/shard_map/ppermute | solution.py:17
  81.7 2.8 %fusion.12 = f32[256,6,128]{0,2,1:T(8,128)} fusion(bf16[256,6,128]{0,2,1:T(8,128)(2,1)} %bitcast.336, f32[6,256,256]{1,2,0:T(8,128)} %copy-done.7, f32[6,256]{1,0:T(8,128)} %copy-done.25, pred[]{:T(512)S(6)} %and.157, f32[256,6]{0,1:T(8,128)} %get-tuple-element.27), kind=kOutput, calls=%fused_computation.42 | convolution fusion | flops 102039552 | bytes 2764801 | tf_op jit(solution)/shard_map/hqk,khe->qhe/dot_general | solution.py:52
  84.5 2.1 %collective-permute-done.14 = bf16[256,768]{0,1:T(8,128)(2,1)} collective-permute-done((bf16[256,768]{0,1:T(8,128)(2,1)}, bf16[256,768]{0,1:T(8,128)(2,1)}, u32[]{:S(2)}, u32[]{:S(2)}) %collective-permute-start.14) | collective-permute-done | bytes 393248 | tf_op jit(solution)/shard_map/ppermute | solution.py:17
  88.6 3.1 %fusion.155 = (f32[6,256]{1,0:T(8,128)}, f32[6,256,256]{1,2,0:T(8,128)}) fusion(bf16[256,6,128]{0,2,1:T(8,128)(2,1)S(1)} %bitcast.325, bf16[256,6,128]{0,2,1:T(8,128)(2,1)} %bitcast.54, pred[]{:T(512)S(6)} %and.173), kind=kOutput, calls=%fused_computation.207 | convolution fusion | flops 101841408 | bytes 2365441 | tf_op jit(solution)/shard_map/qhe,khe->hqk/dot_general | solution.py:45
  91.7 3.6 %collective-permute-start.10 = (bf16[256,768]{0,1:T(8,128)(2,1)}, bf16[256,768]{0,1:T(8,128)(2,1)}, u32[]{:S(2)}, u32[]{:S(2)}) collective-permute-start(bf16[256,768]{0,1:T(8,128)(2,1)} %fusion.59), channel_id=1, source_target_pairs={{4,0},{8,4},{12,8},{16,12},{20,16},{24,20},{28,24},{32,28},{36,32}... | collective-permute-start | bytes 1179656 | tf_op jit(solution)/shard_map/ppermute | solution.py:17
  95.4 1.9 %copy.64 = bf16[256,768]{0,1:T(8,128)(2,1)} copy(bf16[256,768]{1,0:T(8,128)(2,1)} %collective-permute-done.5) | data formatting | bytes 786432 | tf_op jit(solution)/shard_map/ppermute | solution.py:17
  97.3 2.9 %fusion.11 = f32[256,6,128]{0,2,1:T(8,128)} fusion(bf16[256,6,128]{0,2,1:T(8,128)(2,1)} %bitcast.337, f32[6,256,256]{1,2,0:T(8,128)} %copy-done.6, f32[6,256]{1,0:T(8,128)} %copy-done.24, pred[]{:T(512)S(6)} %and.152, f32[256,6]{0,1:T(8,128)} %get-tuple-element.26), kind=kOutput, calls=%fused_computation.41 | convolution fusion | flops 102039552 | bytes 2764801 | tf_op jit(solution)/shard_map/hqk,khe->qhe/dot_general | solution.py:52
  100.1 9.1 %collective-permute-start.8 = (bf16[256,768]{0,1:T(8,128)(2,1)}, bf16[256,768]{0,1:T(8,128)(2,1)}, u32[]{:S(2)}, u32[]{:S(2)}) collective-permute-start(bf16[256,768]{0,1:T(8,128)(2,1)} %fusion.59), channel_id=1, source_target_pairs={{8,0},{12,4},{16,8},{20,12},{24,16},{28,20},{32,24},{36,28},{40,32... | collective-permute-start | bytes 1179656 | tf_op jit(solution)/shard_map/ppermute | solution.py:17
  112.7 1.9 %collective-permute-start.13 = (bf16[256,768]{1,0:T(8,128)(2,1)}, bf16[256,768]{1,0:T(8,128)(2,1)}, u32[]{:S(2)}, u32[]{:S(2)}) collective-permute-start(bf16[256,768]{1,0:T(8,128)(2,1)} %param.14), channel_id=1, source_target_pairs={{0,4},{4,8},{8,12},{12,16},{16,20},{20,24},{24,28},{28,32},{32,36}... | collective-permute-start | bytes 1179656 | tf_op jit(solution)/shard_map/ppermute | solution.py:17
  114.6 1.9 %copy.60 = bf16[256,768]{0,1:T(8,128)(2,1)} copy(bf16[256,768]{1,0:T(8,128)(2,1)} %collective-permute-done.3) | data formatting | bytes 786432 | tf_op jit(solution)/shard_map/ppermute | solution.py:17
  116.5 2.8 %fusion.10 = f32[256,6,128]{0,2,1:T(8,128)} fusion(bf16[256,6,128]{0,2,1:T(8,128)(2,1)} %bitcast.338, f32[6,256,256]{1,2,0:T(8,128)} %copy-done, f32[6,256]{1,0:T(8,128)} %copy-done.17, pred[]{:T(512)S(6)} %and.147, f32[256,6]{0,1:T(8,128)} %get-tuple-element.25), kind=kOutput, calls=%fused_computation.40 | convolution fusion | flops 102039552 | bytes 2764801 | tf_op jit(solution)/shard_map/hqk,khe->qhe/dot_general | solution.py:52
  119.3 3.8 %collective-permute-start.11 = (bf16[256,768]{1,0:T(8,128)(2,1)}, bf16[256,768]{1,0:T(8,128)(2,1)}, u32[]{:S(2)}, u32[]{:S(2)}) collective-permute-start(bf16[256,768]{1,0:T(8,128)(2,1)} %param.14), channel_id=1, source_target_pairs={{4,0},{8,4},{12,8},{16,12},{20,16},{24,20},{28,24},{32,28},{36,32}... | collective-permute-start | bytes 1179656 | tf_op jit(solution)/shard_map/ppermute | solution.py:17
  126.3 5.2 %collective-permute-start.9 = (bf16[256,768]{1,0:T(8,128)(2,1)}, bf16[256,768]{1,0:T(8,128)(2,1)}, u32[]{:S(2)}, u32[]{:S(2)}) collective-permute-start(bf16[256,768]{1,0:T(8,128)(2,1)} %param.14), channel_id=1, source_target_pairs={{8,0},{12,4},{16,8},{20,12},{24,16},{28,20},{32,24},{36,28},{40,32... | collective-permute-start | bytes 1179656 | tf_op jit(solution)/shard_map/ppermute | solution.py:17
  136.4 2.0 %fusion.25 = f32[256,6,128]{0,2,1:T(8,128)} fusion(bf16[256,6,128]{0,2,1:T(8,128)(2,1)S(1)} %bitcast.339, f32[6,256,256]{1,2,0:T(8,128)S(1)} %copy-done.2, f32[6,256]{1,0:T(8,128)S(1)} %copy-done.19, pred[]{:T(512)S(6)} %and.173, f32[256,6]{0,1:T(8,128)} %get-tuple-element.18), kind=kOutput, calls=%fused_computation.55 | convolution fusion | flops 102039552 | bytes 2764801 | tf_op jit(solution)/shard_map/hqk,khe->qhe/dot_general | solution.py:52
  139.5 2.7 %fusion.24 = f32[256,6,128]{0,2,1:T(8,128)} fusion(bf16[256,6,128]{0,2,1:T(8,128)(2,1)S(1)} %bitcast.340, f32[6,256,256]{1,2,0:T(8,128)} %copy-done.5, f32[6,256]{1,0:T(8,128)} %copy-done.22, pred[]{:T(512)S(6)} %and.169, f32[256,6]{0,1:T(8,128)} %get-tuple-element.17), kind=kOutput, calls=%fused_computation.54 | convolution fusion | flops 102039552 | bytes 2764801 | tf_op jit(solution)/shard_map/hqk,khe->qhe/dot_general | solution.py:52
  143.5 3.7 %fusion.47 = bf16[256,6,128]{0,2,1:T(8,128)(2,1)} fusion(f32[256,6,128]{0,2,1:T(8,128)} %fusion.12, f32[256,6,128]{0,2,1:T(8,128)} %fusion.11, f32[256,6,128]{0,2,1:T(8,128)} %fusion.10, f32[256,6,128]{0,2,1:T(8,128)} %fusion, bf16[256,6,128]{0,2,1:T(8,128)(2,1)S(1)} %bitcast.343, f32[6,256,256]{1,2,0:T(8,128)} %copy-done.10, f32[6,256]{1,0:T(8,128)} %copy-done.26, ...), kind=kOutput, calls=%fused_computation.77 | convolution fusion | flops 103809024 | bytes 5541889 | tf_op jit(solution)/shard_map/hqk,khe->qhe/dot_general | solution.py:52
  147.2 1.9 %copy.82 = bf16[256,768]{0,1:T(8,128)(2,1)} copy(bf16[256,768]{1,0:T(8,128)(2,1)} %collective-permute-done.11) | data formatting | bytes 786432 | tf_op jit(solution)/shard_map/ppermute | solution.py:17
  149.1 2.3 %fusion.23 = f32[256,6,128]{0,2,1:T(8,128)} fusion(bf16[256,6,128]{0,2,1:T(8,128)(2,1)} %bitcast.341, f32[6,256,256]{1,2,0:T(8,128)S(1)} %copy-done.4, f32[6,256]{1,0:T(8,128)S(1)} %copy-done.21, pred[]{:T(512)S(6)} %and.165, f32[256,6]{0,1:T(8,128)} %get-tuple-element.16), kind=kOutput, calls=%fused_computation.53 | convolution fusion | flops 102039552 | bytes 2764801 | tf_op jit(solution)/shard_map/hqk,khe->qhe/dot_general | solution.py:52
  151.5 1.9 %copy.92 = bf16[256,768]{1,0:T(8,128)(2,1)} copy(bf16[256,768]{0,1:T(8,128)(2,1)} %bitcast.342) | data formatting | bytes 786432
  153.4 2.1 %fusion.13 = f32[256,6,128]{0,2,1:T(8,128)} fusion(bf16[256,6,128]{0,2,1:T(8,128)(2,1)S(1)} %bitcast.335, f32[6,256,256]{1,2,0:T(8,128)S(1)} %get-tuple-element.57, f32[6,256]{1,0:T(8,128)S(1)} %get-tuple-element.56, pred[]{:T(512)S(6)} %and.137, f32[256,6]{0,1:T(8,128)} %get-tuple-element.15), kind=kOutput, calls=%fused_computation.43 | convolution fusion | flops 102039552 | bytes 2764801 | tf_op jit(solution)/shard_map/hqk,khe->qhe/dot_general | solution.py:52
  156.7 2.4 %fusion.46 = bf16[256,6,128]{0,2,1:T(8,128)(2,1)S(1)} fusion(f32[256,6,128]{0,2,1:T(8,128)} %fusion.25, f32[256,6,128]{0,2,1:T(8,128)} %fusion.24, f32[256,6,128]{0,2,1:T(8,128)} %fusion.23, f32[256,6,128]{0,2,1:T(8,128)} %fusion.13, bf16[256,6,128]{0,2,1:T(8,128)(2,1)S(1)} %bitcast.344, f32[6,256,256]{1,2,0:T(8,128)S(1)} %copy-done.12, ...), kind=kOutput, calls=%fused_computation.76 | convolution fusion | flops 103809024 | bytes 5541889 | tf_op jit(solution)/shard_map/hqk,khe->qhe/dot_general | solution.py:52
  (139 shorter events, 40.7 us)
Async XLA Ops:
  3.2 11.3 %copy-start.35 = (f32[768]{0:T(1024)S(1)}, f32[768]{0:T(1024)}, u32[]{:S(2)}) copy-start(f32[768]{0:T(1024)} %param.19) | copy-start | bytes 9220
  3.5 30.6 %copy-start.33 = (s32[64]{0:T(128)S(1)}, s32[64]{0:T(128)}, u32[]{:S(2)}) copy-start(s32[64]{0:T(128)} %param.23) | copy-start | bytes 772
  3.5 30.5 %copy-start.34 = (s32[64]{0:T(128)S(1)}, s32[64]{0:T(128)}, u32[]{:S(2)}) copy-start(s32[64]{0:T(128)} %param.22) | copy-start | bytes 772
  3.8 44.5 %copy-start.36 = (f32[768]{0:T(1024)S(1)}, f32[768]{0:T(1024)}, u32[]{:S(2)}) copy-start(f32[768]{0:T(1024)} %param.18) | copy-start | bytes 9220
  14.5 34.1 %copy-start.37 = (f32[768]{0:T(1024)S(1)}, f32[768]{0:T(1024)}, u32[]{:S(2)}) copy-start(f32[768]{0:T(1024)} %param.20) | copy-start | bytes 9220
  15.4 38.3 %collective-permute-start.6 = (bf16[256,768]{0,1:T(8,128)(2,1)}, bf16[256,768]{0,1:T(8,128)(2,1)}, u32[]{:S(2)}, u32[]{:S(2)}) collective-permute-start(bf16[256,768]{0,1:T(8,128)(2,1)} %fusion.53), channel_id=1, source_target_pairs={{0,8},{4,12},{8,16},{12,20},{16,24},{20,28},{24,32},{28,36},{32,40... | collective-permute-start | bytes 1179656 | tf_op jit(solution)/shard_map/ppermute | solution.py:17
  18.9 38.5 %collective-permute-start.4 = (bf16[256,768]{0,1:T(8,128)(2,1)}, bf16[256,768]{0,1:T(8,128)(2,1)}, u32[]{:S(2)}, u32[]{:S(2)}) collective-permute-start(bf16[256,768]{0,1:T(8,128)(2,1)} %fusion.53), channel_id=1, source_target_pairs={{0,4},{4,8},{8,12},{12,16},{16,20},{20,24},{24,28},{28,32},{32,36}... | collective-permute-start | bytes 1179656 | tf_op jit(solution)/shard_map/ppermute | solution.py:17
  20.8 41.7 %collective-permute-start.2 = (bf16[256,768]{0,1:T(8,128)(2,1)}, bf16[256,768]{0,1:T(8,128)(2,1)}, u32[]{:S(2)}, u32[]{:S(2)}) collective-permute-start(bf16[256,768]{0,1:T(8,128)(2,1)} %fusion.53), channel_id=1, source_target_pairs={{4,0},{8,4},{12,8},{16,12},{20,16},{24,20},{28,24},{32,28},{36,32}... | collective-permute-start | bytes 1179656 | tf_op jit(solution)/shard_map/ppermute | solution.py:17
  24.5 47.9 %collective-permute-start = (bf16[256,768]{0,1:T(8,128)(2,1)}, bf16[256,768]{0,1:T(8,128)(2,1)}, u32[]{:S(2)}, u32[]{:S(2)}) collective-permute-start(bf16[256,768]{0,1:T(8,128)(2,1)} %fusion.53), channel_id=1, source_target_pairs={{8,0},{12,4},{16,8},{20,12},{24,16},{28,20},{32,24},{36,28},{40,32... | collective-permute-start | bytes 1179656 | tf_op jit(solution)/shard_map/ppermute | solution.py:17
  30.2 47.7 %collective-permute-start.7 = (bf16[256,768]{1,0:T(8,128)(2,1)}, bf16[256,768]{1,0:T(8,128)(2,1)}, u32[]{:S(2)}, u32[]{:S(2)}) collective-permute-start(bf16[256,768]{1,0:T(8,128)(2,1)} %param.17), channel_id=1, source_target_pairs={{0,8},{4,12},{8,16},{12,20},{16,24},{20,28},{24,32},{28,36},{32,40... | collective-permute-start | bytes 1179656 | tf_op jit(solution)/shard_map/ppermute | solution.py:17
  32.1 16.7 %copy-start.38 = (f32[768]{0:T(1024)S(1)}, f32[768]{0:T(1024)}, u32[]{:S(2)}) copy-start(f32[768]{0:T(1024)} %param.21) | copy-start | bytes 9220
  53.8 38.0 %collective-permute-start.5 = (bf16[256,768]{1,0:T(8,128)(2,1)}, bf16[256,768]{1,0:T(8,128)(2,1)}, u32[]{:S(2)}, u32[]{:S(2)}) collective-permute-start(bf16[256,768]{1,0:T(8,128)(2,1)} %param.17), channel_id=1, source_target_pairs={{0,4},{4,8},{8,12},{12,16},{16,20},{20,24},{24,28},{28,32},{32,36}... | collective-permute-start | bytes 1179656 | tf_op jit(solution)/shard_map/ppermute | solution.py:17
  57.1 20.0 %copy-start.25 = (f32[6,256]{1,0:T(8,128)}, f32[6,256]{1,0:T(8,128)S(1)}, u32[]{:S(2)}) copy-start(f32[6,256]{1,0:T(8,128)S(1)} %get-tuple-element.38) | copy-start | bytes 18436
  57.4 55.2 %collective-permute-start.3 = (bf16[256,768]{1,0:T(8,128)(2,1)}, bf16[256,768]{1,0:T(8,128)(2,1)}, u32[]{:S(2)}, u32[]{:S(2)}) collective-permute-start(bf16[256,768]{1,0:T(8,128)(2,1)} %param.17), channel_id=1, source_target_pairs={{4,0},{8,4},{12,8},{16,12},{20,16},{24,20},{28,24},{32,28},{36,32}... | collective-permute-start | bytes 1179656 | tf_op jit(solution)/shard_map/ppermute | solution.py:17
  62.5 9.0 %copy-start.6 = (f32[6,256,256]{1,2,0:T(8,128)}, f32[6,256,256]{1,2,0:T(8,128)S(1)}, u32[]{:S(2)}) copy-start(f32[6,256,256]{1,2,0:T(8,128)S(1)} %get-tuple-element.41) | copy-start | bytes 4718596
  62.5 14.6 %copy-start.24 = (f32[6,256]{1,0:T(8,128)}, f32[6,256]{1,0:T(8,128)S(1)}, u32[]{:S(2)}) copy-start(f32[6,256]{1,0:T(8,128)S(1)} %get-tuple-element.40) | copy-start | bytes 18436
  62.6 79.7 %collective-permute-start.1 = (bf16[256,768]{1,0:T(8,128)(2,1)}, bf16[256,768]{1,0:T(8,128)(2,1)}, u32[]{:S(2)}, u32[]{:S(2)}) collective-permute-start(bf16[256,768]{1,0:T(8,128)(2,1)} %param.17), channel_id=1, source_target_pairs={{8,0},{12,4},{16,8},{20,12},{24,16},{28,20},{32,24},{36,28},{40,32... | collective-permute-start | bytes 1179656 | tf_op jit(solution)/shard_map/ppermute | solution.py:17
  71.3 5.9 %copy-start.17 = (f32[6,256]{1,0:T(8,128)}, f32[6,256]{1,0:T(8,128)S(1)}, u32[]{:S(2)}) copy-start(f32[6,256]{1,0:T(8,128)S(1)} %get-tuple-element.42) | copy-start | bytes 18436
  72.4 14.3 %collective-permute-start.14 = (bf16[256,768]{0,1:T(8,128)(2,1)}, bf16[256,768]{0,1:T(8,128)(2,1)}, u32[]{:S(2)}, u32[]{:S(2)}) collective-permute-start(bf16[256,768]{0,1:T(8,128)(2,1)} %fusion.59), channel_id=1, source_target_pairs={{0,8},{4,12},{8,16},{12,20},{16,24},{20,28},{24,32},{28,36},{32,40... | collective-permute-start | bytes 1179656 | tf_op jit(solution)/shard_map/ppermute | solution.py:17
  77.9 57.3 %collective-permute-start.15 = (bf16[256,768]{1,0:T(8,128)(2,1)}, bf16[256,768]{1,0:T(8,128)(2,1)}, u32[]{:S(2)}, u32[]{:S(2)}) collective-permute-start(bf16[256,768]{1,0:T(8,128)(2,1)} %param.14), channel_id=1, source_target_pairs={{0,8},{4,12},{8,16},{12,20},{16,24},{20,28},{24,32},{28,36},{32,40... | collective-permute-start | bytes 1179656 | tf_op jit(solution)/shard_map/ppermute | solution.py:17
  86.7 13.5 %collective-permute-start.12 = (bf16[256,768]{0,1:T(8,128)(2,1)}, bf16[256,768]{0,1:T(8,128)(2,1)}, u32[]{:S(2)}, u32[]{:S(2)}) collective-permute-start(bf16[256,768]{0,1:T(8,128)(2,1)} %fusion.59), channel_id=1, source_target_pairs={{0,4},{4,8},{8,12},{12,16},{16,20},{20,24},{24,28},{28,32},{32,36}... | collective-permute-start | bytes 1179656 | tf_op jit(solution)/shard_map/ppermute | solution.py:17
  91.7 27.6 %collective-permute-start.10 = (bf16[256,768]{0,1:T(8,128)(2,1)}, bf16[256,768]{0,1:T(8,128)(2,1)}, u32[]{:S(2)}, u32[]{:S(2)}) collective-permute-start(bf16[256,768]{0,1:T(8,128)(2,1)} %fusion.59), channel_id=1, source_target_pairs={{4,0},{8,4},{12,8},{16,12},{20,16},{24,20},{28,24},{32,28},{36,32}... | collective-permute-start | bytes 1179656 | tf_op jit(solution)/shard_map/ppermute | solution.py:17
  100.1 10.6 %copy-start.1 = (f32[6,256,256]{1,2,0:T(8,128)S(1)}, f32[6,256,256]{1,2,0:T(8,128)}, u32[]{:S(2)}) copy-start(f32[6,256,256]{1,2,0:T(8,128)} %get-tuple-element.49) | copy-start | bytes 4718596
  100.1 10.6 %copy-start.18 = (f32[6,256]{1,0:T(8,128)S(1)}, f32[6,256]{1,0:T(8,128)}, u32[]{:S(2)}) copy-start(f32[6,256]{1,0:T(8,128)} %get-tuple-element.48) | copy-start | bytes 18436
  100.1 26.1 %collective-permute-start.8 = (bf16[256,768]{0,1:T(8,128)(2,1)}, bf16[256,768]{0,1:T(8,128)(2,1)}, u32[]{:S(2)}, u32[]{:S(2)}) collective-permute-start(bf16[256,768]{0,1:T(8,128)(2,1)} %fusion.59), channel_id=1, source_target_pairs={{8,0},{12,4},{16,8},{20,12},{24,16},{28,20},{32,24},{36,28},{40,32... | collective-permute-start | bytes 1179656 | tf_op jit(solution)/shard_map/ppermute | solution.py:17
  112.7 25.7 %collective-permute-start.13 = (bf16[256,768]{1,0:T(8,128)(2,1)}, bf16[256,768]{1,0:T(8,128)(2,1)}, u32[]{:S(2)}, u32[]{:S(2)}) collective-permute-start(bf16[256,768]{1,0:T(8,128)(2,1)} %param.14), channel_id=1, source_target_pairs={{0,4},{4,8},{8,12},{12,16},{16,20},{20,24},{24,28},{28,32},{32,36}... | collective-permute-start | bytes 1179656 | tf_op jit(solution)/shard_map/ppermute | solution.py:17
  119.3 27.9 %collective-permute-start.11 = (bf16[256,768]{1,0:T(8,128)(2,1)}, bf16[256,768]{1,0:T(8,128)(2,1)}, u32[]{:S(2)}, u32[]{:S(2)}) collective-permute-start(bf16[256,768]{1,0:T(8,128)(2,1)} %param.14), channel_id=1, source_target_pairs={{4,0},{8,4},{12,8},{16,12},{20,16},{24,20},{28,24},{32,28},{36,32}... | collective-permute-start | bytes 1179656 | tf_op jit(solution)/shard_map/ppermute | solution.py:17
  124.6 9.9 %copy-start.20 = (f32[6,256]{1,0:T(8,128)}, f32[6,256]{1,0:T(8,128)S(1)}, u32[]{:S(2)}) copy-start(f32[6,256]{1,0:T(8,128)S(1)} %get-tuple-element.52) | copy-start | bytes 18436
  126.3 29.3 %collective-permute-start.9 = (bf16[256,768]{1,0:T(8,128)(2,1)}, bf16[256,768]{1,0:T(8,128)(2,1)}, u32[]{:S(2)}, u32[]{:S(2)}) collective-permute-start(bf16[256,768]{1,0:T(8,128)(2,1)} %param.14), channel_id=1, source_target_pairs={{8,0},{12,4},{16,8},{20,12},{24,16},{28,20},{32,24},{36,28},{40,32... | collective-permute-start | bytes 1179656 | tf_op jit(solution)/shard_map/ppermute | solution.py:17
  143.5 5.7 %copy-start.4 = (f32[6,256,256]{1,2,0:T(8,128)S(1)}, f32[6,256,256]{1,2,0:T(8,128)}, u32[]{:S(2)}) copy-start(f32[6,256,256]{1,2,0:T(8,128)} %copy-done.3) | copy-start | bytes 4718596
  143.5 5.7 %copy-start.21 = (f32[6,256]{1,0:T(8,128)S(1)}, f32[6,256]{1,0:T(8,128)}, u32[]{:S(2)}) copy-start(f32[6,256]{1,0:T(8,128)} %copy-done.20) | copy-start | bytes 18436
  149.1 4.3 %copy-start.14 = (bf16[256,768]{0,1:T(8,128)(2,1)S(1)}, bf16[256,768]{0,1:T(8,128)(2,1)}, u32[]{:S(2)}) copy-start(bf16[256,768]{0,1:T(8,128)(2,1)} %copy.74) | copy-start | bytes 1179652
  (23 other events, 55.9 us)
where the time goes:
time: 162 us; the launch traced here: 160 us
  starting transfers between devices  58.9 us (36%)
  matrix products  41.2 us (25%)
  local copies, waits for them, and re-layouts  25.4 us (16%)
  between operations  13.2 us (8%)
  blocking collectives  10.5 us (6%)
  other arithmetic  8.74 us (5%)
  waiting for transfers between devices  2.15 us (1%)
    ppermute x16, starting transfers between devices, shifted(): return lax.ppermute(array, axis, pairs)  58.9 us
    dot_general x10, matrix products, partial_attend(): jnp.einsum('hqk,khe->qhe', weights.astype(jnp.bfloat16), vh, preferred_el...  25.1 us
    dot_general x10, matrix products, partial_attend(): jnp.einsum('qhe,khe->hqk', qh, kh, preferred_element_type=jnp.float32)  16.1 us
    unnamed x86, local copies, waits for them, and re-layouts  12.4 us
    ppermute x8, local copies, waits for them, and re-layouts, shifted(): return lax.ppermute(array, axis, pairs)  12.3 us
    psum x1, blocking collectives, local(): lax.psum((squares(video_q), squares(audio_k), squares(audio_q), squares(v...  10.5 us
    reduce_sum x10, other arithmetic, partial_attend(): total = jnp.sum(weights, axis=2)  4.69 us
  transfers between devices with their start and end apart: 16, of which 1 were waited for; matrix products, arithmetic and copies ran while one was open for 40% of the time, Pallas kernels for 0%

commit v1 on v0

v1 whole, which is shorter than its diff:
```python
import jax
import jax.numpy as jnp
from jax import lax
from jax.experimental import pallas as pl
from jax.experimental.pallas import tpu as pltpu
from jax.sharding import PartitionSpec as P

HEAD_DIM = 128
EPS = 1e-06
NEG = -1e30
MESH = pl.DeviceIdType.MESH
LOG2E = 1.4426950408889634

PARTNER, DIRECT, NEAR, FAR = 0, 1, 2, 3
OFFSET = (1, -2, -1, 2)
AUDIO, VIDEO = 0, 1


def kernel(
    count_seq,
    count_head,
    vq_hbm,
    vk_hbm,
    vv_hbm,
    aq_hbm,
    ak_hbm,
    av_hbm,
    vqg,
    akg,
    aqg,
    vkg,
    first_ref,
    count_ref,
    vout,
    aout,
    raw,
    own_v,
    nq,
    nk,
    far_k,
    far_v,
    sums,
    sums_in,
    local_sem,
    sum_send,
    sum_recv,
    v_send,
    v_recv,
    k_send,
    k_recv,
):
    seq = lax.axis_index("seq")
    head = lax.axis_index("head")
    sigma = 1 - 2 * lax.rem(seq, 2)
    heads = nk.shape[1]
    rows = raw.shape[1]
    width = raw.shape[2] * count_head

    def at(by):
        return lax.rem(seq + by * sigma + count_seq, count_seq)

    loads = []
    for i, ref in enumerate((ak_hbm, vk_hbm, vq_hbm, aq_hbm)):
        loads.append(pltpu.make_async_copy(ref, raw.at[i], local_sem.at[i]))
    for i, ref in enumerate((av_hbm, vv_hbm)):
        loads.append(pltpu.make_async_copy(ref, own_v.at[i], local_sem.at[4 + i]))
    for load in loads:
        load.start()

    barrier = pltpu.get_barrier_semaphore()
    for by in (1, 2, -1, -2):
        pl.semaphore_signal(barrier, inc=1, device_id=(at(by), head), device_id_type=MESH)
    for by in range(1, count_head):
        pl.semaphore_signal(
            barrier, inc=1, device_id=(seq, lax.rem(head + by, count_head)), device_id_type=MESH
        )
    pl.semaphore_wait(barrier, 4 + count_head - 1)

    def target(slot, mod):
        if (slot, mod) in ((FAR, AUDIO), (NEAR, VIDEO)):
            return at(1)
        return at({PARTNER: 1, DIRECT: 2, NEAR: -1, FAR: -2}[slot])

    def v_copy(slot, mod):
        if (slot, mod) == (FAR, AUDIO):
            src = far_v.at[NEAR, AUDIO]
        elif (slot, mod) == (NEAR, VIDEO):
            src = far_v.at[FAR, VIDEO]
        else:
            src = (av_hbm, vv_hbm)[mod]
        return pltpu.make_async_remote_copy(
            src_ref=src,
            dst_ref=far_v.at[slot, mod],
            send_sem=v_send.at[slot, mod],
            recv_sem=v_recv.at[slot, mod],
            device_id=(target(slot, mod), head),
            device_id_type=MESH,
        )

    def k_copy(slot, mod, h):
        if (slot, mod) == (FAR, AUDIO):
            src = far_k.at[NEAR, AUDIO, h]
        elif (slot, mod) == (NEAR, VIDEO):
            src = far_k.at[FAR, VIDEO, h]
        else:
            src = nk.at[mod, h]
        return pltpu.make_async_remote_copy(
            src_ref=src,
            dst_ref=far_k.at[slot, mod, h],
            send_sem=k_send.at[slot, mod, h],
            recv_sem=k_recv.at[slot, mod, h],
            device_id=(target(slot, mod), head),
            device_id_type=MESH,
        )

    sends = ((NEAR, AUDIO), (FAR, VIDEO), (DIRECT, AUDIO), (DIRECT, VIDEO), (PARTNER, AUDIO), (PARTNER, VIDEO))
    relays = ((FAR, AUDIO), (NEAR, VIDEO))
    for slot, mod in sends:
        v_copy(slot, mod).start()

    lane = lax.broadcasted_iota(jnp.int32, (rows, HEAD_DIM), 1)
    packed = jnp.zeros((rows, HEAD_DIM), jnp.float32)
    for i in range(4):
        loads[i].wait()
        total = jnp.zeros((rows, HEAD_DIM), jnp.float32)
        for h in range(heads):
            wide = raw[i, :, h * HEAD_DIM : (h + 1) * HEAD_DIM].astype(jnp.float32)
            total += wide * wide
        packed = jnp.where(lane == i, jnp.sum(total, axis=1, keepdims=True), packed)
    sums[...] = jnp.transpose(packed)[:8]

    def sum_copy(by):
        return pltpu.make_async_remote_copy(
            src_ref=sums,
            dst_ref=sums_in.at[by - 1],
            send_sem=sum_send.at[by - 1],
            recv_sem=sum_recv.at[by - 1],
            device_id=(seq, lax.rem(head + by, count_head)),
            device_id_type=MESH,
        )

    for by in range(1, count_head):
        sum_copy(by).start()
    all_sums = sums[...]
    for by in range(1, count_head):
        sum_copy(by).wait_recv()
        all_sums += sums_in[by - 1]
    scale = lax.rsqrt(all_sums / width + EPS)
    scale = jnp.transpose(jnp.concatenate([scale] * (HEAD_DIM // 8), axis=0))

    def normalized(i, gain, h):
        cols = slice(h * HEAD_DIM, (h + 1) * HEAD_DIM)
        wide = raw[i, :, cols].astype(jnp.float32)
        return (wide * scale[:, i : i + 1] * gain[cols]).astype(jnp.bfloat16)

    for h in range(heads):
        nk[AUDIO, h] = normalized(0, akg, h)
        nk[VIDEO, h] = normalized(1, vkg, h)
        for slot, mod in sends:
            k_copy(slot, mod, h).start()
    for h in range(heads):
        nq[VIDEO, h] = normalized(2, vqg, h)
        nq[AUDIO, h] = normalized(3, aqg, h)
    loads[4].wait()
    loads[5].wait()

    def covers(stretch, tile):
        safe = lax.rem(stretch + count_seq, count_seq)
        first = first_ref[safe]
        inside = (stretch >= 0) & (stretch < count_seq) & (tile >= 0) & (tile < count_seq)
        return inside & (tile >= first) & (tile < first + count_ref[safe])

    bias = ([], [])
    for slot in range(4):
        other = seq + OFFSET[slot] * sigma
        bias[VIDEO].append(jnp.where(covers(other, seq), 0.0, NEG))
        bias[AUDIO].append(jnp.where(covers(seq, other), 0.0, NEG))

    factor = LOG2E * HEAD_DIM**-0.5

    def attend(q_mod, h):
        k_mod = 1 - q_mod
        cols = pl.ds(pl.multiple_of(h * HEAD_DIM, HEAD_DIM), HEAD_DIM)
        query = nq[q_mod, h]
        keys = [nk[k_mod, h]] + [far_k[slot, k_mod, h] for slot in range(4)]
        values = [own_v[k_mod, :, cols]] + [far_v[slot, k_mod, :, cols] for slot in range(4)]
        off = [0.0] + bias[q_mod]
        scores, top = [], None
        for key, add in zip(keys, off):
            score = lax.dot_general(
                query, key, (((1,), (1,)), ((), ())), preferred_element_type=jnp.float32
            )
            scores.append(score)
            most = jnp.max(score, axis=1, keepdims=True) + add
            top = most if top is None else jnp.maximum(top, most)
        total = jnp.zeros((rows, 1), jnp.float32)
        mixed = jnp.zeros((rows, HEAD_DIM), jnp.float32)
        for score, value, add in zip(scores, values, off):
            weights = jnp.exp2((score - (top - add)) * factor)
            total += jnp.sum(weights, axis=1, keepdims=True)
            mixed += jnp.dot(
                weights.astype(jnp.bfloat16), value, preferred_element_type=jnp.float32
            )
        return (mixed / total).astype(jnp.bfloat16), cols

    for slot, mod in ((NEAR, AUDIO), (FAR, VIDEO)):
        v_copy(slot, mod).wait_recv()
    for slot, mod in relays:
        v_copy(slot, mod).start()
    for slot, mod in ((PARTNER, AUDIO), (PARTNER, VIDEO), (DIRECT, AUDIO), (DIRECT, VIDEO)) + relays:
        v_copy(slot, mod).wait_recv()

    def forward(h):
        for slot, mod in ((NEAR, AUDIO), (FAR, VIDEO)):
            k_copy(slot, mod, h).wait_recv()
        for slot, mod in relays:
            k_copy(slot, mod, h).start()

    forward(0)

    def body(h, carry):
        @pl.when(h < heads - 1)
        def _():
            forward(h + 1)

        for slot, mod in ((PARTNER, AUDIO), (PARTNER, VIDEO), (DIRECT, AUDIO), (DIRECT, VIDEO)) + relays:
            k_copy(slot, mod, h).wait_recv()
        result, cols = attend(VIDEO, h)
        vout[:, cols] = result
        result, cols = attend(AUDIO, h)
        aout[:, cols] = result
        return carry

    lax.fori_loop(0, heads, body, 0)

    for by in range(1, count_head):
        sum_copy(by).wait_send()
    for slot, mod in sends + relays:
        v_copy(slot, mod).wait_send()

    def drain(h, carry):
        for slot, mod in sends + relays:
            k_copy(slot, mod, h).wait_send()
        return carry

    lax.fori_loop(0, heads, drain, 0)


def local(
    video_q,
    video_k,
    video_v,
    audio_q,
    audio_k,
    audio_v,
    video_q_gain,
    audio_k_gain,
    audio_q_gain,
    video_k_gain,
    tile_first,
    tile_count,
):
    count_seq, count_head = lax.axis_size("seq"), lax.axis_size("head")
    rows, cols = video_q.shape
    heads = cols // HEAD_DIM
    gains = (video_q_gain, audio_k_gain, audio_q_gain, video_k_gain)

    def body(*refs):
        kernel(count_seq, count_head, *refs)

    hbm = pl.BlockSpec(memory_space=pl.ANY)
    vmem = pl.BlockSpec(memory_space=pltpu.VMEM)
    smem = pl.BlockSpec(memory_space=pltpu.SMEM)
    return pl.pallas_call(
        body,
        out_shape=(
            jax.ShapeDtypeStruct((rows, cols), jnp.bfloat16),
            jax.ShapeDtypeStruct((rows, cols), jnp.bfloat16),
        ),
        in_specs=[hbm] * 6 + [vmem] * 4 + [smem] * 2,
        out_specs=(vmem, vmem),
        scratch_shapes=[
            pltpu.VMEM((4, rows, cols), jnp.bfloat16),
            pltpu.VMEM((2, rows, cols), jnp.bfloat16),
            pltpu.VMEM((2, heads, rows, HEAD_DIM), jnp.bfloat16),
            pltpu.VMEM((2, heads, rows, HEAD_DIM), jnp.bfloat16),
            pltpu.VMEM((4, 2, heads, rows, HEAD_DIM), jnp.bfloat16),
            pltpu.VMEM((4, 2, rows, cols), jnp.bfloat16),
            pltpu.VMEM((8, rows), jnp.float32),
            pltpu.VMEM((count_head - 1, 8, rows), jnp.float32),
            pltpu.SemaphoreType.DMA((6,)),
            pltpu.SemaphoreType.DMA((count_head - 1,)),
            pltpu.SemaphoreType.DMA((count_head - 1,)),
            pltpu.SemaphoreType.DMA((4, 2)),
            pltpu.SemaphoreType.DMA((4, 2)),
            pltpu.SemaphoreType.DMA((4, 2, heads)),
            pltpu.SemaphoreType.DMA((4, 2, heads)),
        ],
        compiler_params=pltpu.CompilerParams(
            collective_id=0, has_side_effects=True, vmem_limit_bytes=56 * 1024 * 1024
        ),
        name="attend",
    )(video_q, video_k, video_v, audio_q, audio_k, audio_v, *gains, tile_first, tile_count)


def solution(mesh):
    return jax.shard_map(
        local,
        mesh=mesh,
        in_specs=(P("seq", "head"),) * 6 + (P("head"),) * 4 + (P(), P()),
        out_specs=(P("seq", "head"), P("seq", "head")),
        check_vma=False,
    )
```

time: 162 us -> 54.8 us (0.34)
  the two profiles are of different devices: /device:TPU:136 before, /device:TPU:1 now
where the time goes in v1:
time: 54.8 us; the launch traced here: 54.7 us
  Pallas kernels  51.4 us (94%)
  local copies, waits for them, and re-layouts  2.57 us (5%)
  between operations  0.65 us (1%)
    pallas_call x1, Pallas kernels, local(): pl.pallas_call(body, out_shape=(jax.ShapeDtypeStruct((rows, cols), jnp.bf...  51.4 us
    unnamed x4, local copies, waits for them, and re-layouts  2.57 us

profile of v1, /device:TPU:1, one launch (start us, length us, event | category | flops | bytes accessed | tf_op | source)
XLA Modules:
  0.0 54.7 jit_solution(15031518505773608724)
XLA Ops:
  0.6 51.4 %attend.1 = (bf16[256,768]{1,0:T(8,128)(2,1)}, bf16[256,768]{1,0:T(8,128)(2,1)}) custom-call(bf16[256,768]{1,0:T(8,128)(2,1)} %refs_0_.1, bf16[256,768]{1,0:T(8,128)(2,1)} %refs_1_.1, bf16[256,768]{1,0:T(8,128)(2,1)} %refs_2_.1, bf16[256,768]{1,0:T(8,128)(2,1)} %refs_3_.1, bf16[256,768]{1,0:T(8,128)(2,1)} %refs_4_.1, bf16[256,768]{1,0:T(8,128)(2,1)} %refs_5_.1, ...), custom_call_target="tpu_custom_call" | custom-call | tf_op jit(solution)/shard_map/attend/pallas_call | solution.py:274
  52.1 0.0 copy-start
  52.1 1.8 %copy.16 = bf16[256,768]{1,0:T(8,128)(2,1)} copy(bf16[256,768]{1,0:T(8,128)(2,1)} %get-tuple-element.4) | data formatting | bytes 786432
  53.9 0.0 copy-done
  53.9 0.7 %copy.17 = bf16[256,768]{1,0:T(8,128)(2,1)} copy(bf16[256,768]{1,0:T(8,128)(2,1)S(1)} %copy-done) | data formatting | bytes 786432
Async XLA Ops:
  52.1 1.8 %copy-start = (bf16[256,768]{1,0:T(8,128)(2,1)S(1)}, bf16[256,768]{1,0:T(8,128)(2,1)}, u32[]{:S(2)}) copy-start(bf16[256,768]{1,0:T(8,128)(2,1)} %get-tuple-element.5) | copy-start | bytes 1179652

commit v2 on v1

v2 whole, which is shorter than its diff:
```python
import jax
import jax.numpy as jnp
from jax import lax
from jax.experimental import pallas as pl
from jax.experimental.pallas import tpu as pltpu
from jax.sharding import PartitionSpec as P

HEAD_DIM = 128
EPS = 1e-06
NEG = -1e30
MESH = pl.DeviceIdType.MESH
LOG2E = 1.4426950408889634
FACTOR = LOG2E * HEAD_DIM**-0.5

PARTNER, DIRECT, NEAR, FAR = 0, 1, 2, 3
OFFSET = (1, -2, -1, 2)
AUDIO, VIDEO = 0, 1
KEY, VALUE = 0, 1
SPLIT = ((NEAR, AUDIO), (FAR, VIDEO))
RELAY = ((FAR, AUDIO), (NEAR, VIDEO))


def kernel(
    count_seq,
    count_head,
    vq_hbm,
    vk_hbm,
    vv_hbm,
    aq_hbm,
    ak_hbm,
    av_hbm,
    vqg,
    akg,
    aqg,
    vkg,
    first_ref,
    count_ref,
    vout,
    aout,
    raw,
    raw_v,
    own,
    nq,
    far,
    top_ref,
    total_ref,
    mixed_ref,
    sums,
    sums_in,
    local_sem,
    value_sem,
    sum_send,
    sum_recv,
    partner_send,
    partner_recv,
    split_send,
    split_recv,
    relay_send,
    relay_recv,
    direct_send,
    direct_recv,
):
    seq = lax.axis_index("seq")
    head = lax.axis_index("head")
    sigma = 1 - 2 * lax.rem(seq, 2)
    heads = nq.shape[0]
    rows = raw.shape[1]
    width = raw.shape[2] * count_head
    behind = (seq - sigma >= 0) & (seq - sigma < count_seq)
    ahead = (seq + 2 * sigma >= 0) & (seq + 2 * sigma < count_seq)

    loads = []
    for i, ref in enumerate((ak_hbm, vk_hbm, vq_hbm, aq_hbm)):
        loads.append(pltpu.make_async_copy(ref, raw.at[i], local_sem.at[i]))
    value_loads = []
    for mod, ref in enumerate((av_hbm, vv_hbm)):
        for h in range(heads):
            value_loads.append(
                pltpu.make_async_copy(
                    ref.at[:, pl.ds(h * HEAD_DIM, HEAD_DIM)],
                    raw_v.at[h, mod],
                    value_sem.at[mod, h],
                )
            )
    barrier = pltpu.get_barrier_semaphore()

    def greet(by):
        pl.semaphore_signal(barrier, inc=1, device_id=(seq + by * sigma, head), device_id_type=MESH)

    greet(1)
    for by in range(1, count_head):
        pl.semaphore_signal(
            barrier, inc=1, device_id=(seq, lax.rem(head + by, count_head)), device_id_type=MESH
        )

    @pl.when(behind)
    def _():
        greet(-1)
        greet(-2)

    @pl.when(ahead)
    def _():
        greet(2)

    for load in value_loads + loads:
        load.start()
    for load in value_loads:
        load.wait()
    for h in range(heads):
        for mod in (AUDIO, VIDEO):
            for r in range(0, rows, HEAD_DIM):
                own[h, mod, VALUE, r : r + HEAD_DIM] = jnp.transpose(raw_v[h, mod, r : r + HEAD_DIM])
    peers = count_head + 2 * behind.astype(jnp.int32) + ahead.astype(jnp.int32)
    pl.semaphore_wait(barrier, peers)

    def remote(src, dst, send, recv, by):
        return pltpu.make_async_remote_copy(
            src_ref=src,
            dst_ref=dst,
            send_sem=send,
            recv_sem=recv,
            device_id=(seq + by * sigma, head),
            device_id_type=MESH,
        )

    def block(ref, mod, part):
        if isinstance(part, int) and part == 0:
            return ref.at[:, mod, VALUE]
        return ref.at[part - 1, mod, KEY]

    def split_copy(slot, mod, part):
        by = -1 if slot == NEAR else -2
        return remote(
            block(own, mod, part),
            block(far.at[slot], mod, part),
            split_send.at[mod, part],
            split_recv.at[mod, part],
            by,
        )

    def relay_copy(slot, mod, part):
        held = NEAR if slot == FAR else FAR
        return remote(
            block(far.at[held], mod, part),
            block(far.at[slot], mod, part),
            relay_send.at[mod, part],
            relay_recv.at[mod, part],
            1,
        )

    def partner_copy(kv):
        return remote(own.at[:, :, kv], far.at[PARTNER, :, :, kv], partner_send.at[kv], partner_recv.at[kv], 1)

    def direct_copy(h):
        return remote(own.at[h], far.at[DIRECT, h], direct_send.at[h], direct_recv.at[h], 2)

    def start_split(part):
        @pl.when(behind)
        def _():
            for slot, mod in SPLIT:
                split_copy(slot, mod, part).start()

    def start_relay(part):
        @pl.when(behind)
        def _():
            split_copy(NEAR, AUDIO, part).wait_recv()
            relay_copy(FAR, AUDIO, part).start()

        @pl.when(ahead)
        def _():
            split_copy(FAR, VIDEO, part).wait_recv()
            relay_copy(NEAR, VIDEO, part).start()

    def finish_relay(part):
        @pl.when(ahead)
        def _():
            relay_copy(FAR, AUDIO, part).wait_recv()

        @pl.when(behind)
        def _():
            relay_copy(NEAR, VIDEO, part).wait_recv()

    start_split(0)
    partner_copy(VALUE).start()

    def clear(slot):
        def body(h, carry):
            far[slot, h] = jnp.zeros(far.shape[2:], far.dtype)
            return carry

        lax.fori_loop(0, heads, body, 0)

    @pl.when(jnp.logical_not(behind))
    def _():
        clear(DIRECT)
        clear(NEAR)

    @pl.when(jnp.logical_not(ahead))
    def _():
        clear(FAR)

    lane = lax.broadcasted_iota(jnp.int32, (rows, HEAD_DIM), 1)
    packed = jnp.zeros((rows, HEAD_DIM), jnp.float32)
    for i in range(4):
        loads[i].wait()
        total = jnp.zeros((rows, HEAD_DIM), jnp.float32)
        for h in range(heads):
            wide = raw[i, :, h * HEAD_DIM : (h + 1) * HEAD_DIM].astype(jnp.float32)
            total += wide * wide
        packed = jnp.where(lane == i, jnp.sum(total, axis=1, keepdims=True), packed)
    sums[...] = jnp.transpose(packed)[:8]

    def sum_copy(by):
        return pltpu.make_async_remote_copy(
            src_ref=sums,
            dst_ref=sums_in.at[by - 1],
            send_sem=sum_send.at[by - 1],
            recv_sem=sum_recv.at[by - 1],
            device_id=(seq, lax.rem(head + by, count_head)),
            device_id_type=MESH,
        )

    for by in range(1, count_head):
        sum_copy(by).start()
    all_sums = sums[...]
    for by in range(1, count_head):
        sum_copy(by).wait_recv()
        all_sums += sums_in[by - 1]
    scale = lax.rsqrt(all_sums / width + EPS)
    scale = jnp.transpose(jnp.concatenate([scale] * (HEAD_DIM // 8), axis=0))

    def normalized(i, gain, h):
        cols = slice(h * HEAD_DIM, (h + 1) * HEAD_DIM)
        wide = raw[i, :, cols].astype(jnp.float32)
        return (wide * scale[:, i : i + 1] * gain[cols]).astype(jnp.bfloat16)

    for h in range(heads):
        own[h, AUDIO, KEY] = normalized(0, akg, h)
        own[h, VIDEO, KEY] = normalized(1, vkg, h)
        start_split(h + 1)

        @pl.when(ahead)
        def _():
            direct_copy(h).start()

    partner_copy(KEY).start()
    for h in range(heads):
        nq[h, VIDEO] = normalized(2, vqg, h)
        nq[h, AUDIO] = normalized(3, aqg, h)

    def covers(stretch, tile):
        safe = lax.rem(stretch + count_seq, count_seq)
        first = first_ref[safe]
        inside = (stretch >= 0) & (stretch < count_seq) & (tile >= 0) & (tile < count_seq)
        return inside & (tile >= first) & (tile < first + count_ref[safe])

    bias = ([], [])
    for slot in range(4):
        other = seq + OFFSET[slot] * sigma
        bias[VIDEO].append(jnp.where(covers(other, seq), 0.0, NEG))
        bias[AUDIO].append(jnp.where(covers(seq, other), 0.0, NEG))

    def attend(h, slots, opening=False, closing=False):
        jobs = []
        for q_mod in (VIDEO, AUDIO):
            refs = [(far.at[slot, h, 1 - q_mod], bias[q_mod][slot]) for slot in slots]
            if opening:
                refs.insert(0, (own.at[h, 1 - q_mod], 0.0))
            query = nq[h, q_mod]
            scores = [
                lax.dot_general(
                    ref[KEY], query, (((1,), (1,)), ((), ())), preferred_element_type=jnp.float32
                )
                for ref, _ in refs
            ]
            jobs.append((q_mod, refs, scores))
        tops = []
        for q_mod, refs, scores in jobs:
            top = None if opening else top_ref[h, q_mod]
            for score, (_, add) in zip(scores, refs):
                most = jnp.max(score, axis=0, keepdims=True) + add
                top = most if top is None else jnp.maximum(top, most)
            tops.append(top)
        results = []
        for (q_mod, refs, scores), top in zip(jobs, tops):
            total, mixed = None, None
            for score, (ref, add) in zip(scores, refs):
                weights = jnp.exp2((score - (top - add)) * FACTOR)
                part = jnp.sum(weights, axis=0, keepdims=True)
                value = jnp.concatenate(
                    [ref[VALUE, r : r + HEAD_DIM] for r in range(0, rows, HEAD_DIM)], axis=1
                )
                block = jnp.dot(
                    value, weights.astype(jnp.bfloat16), preferred_element_type=jnp.float32
                )
                total = part if total is None else total + part
                mixed = block if mixed is None else mixed + block
            if not opening:
                fade = jnp.exp2((top_ref[h, q_mod] - top) * FACTOR)
                total += total_ref[h, q_mod] * fade
                mixed += mixed_ref[h, q_mod] * fade
            results.append((q_mod, top, total, mixed))
        if closing:
            return [jnp.transpose(mixed / total).astype(jnp.bfloat16) for _, _, total, mixed in results]
        for q_mod, top, total, mixed in results:
            top_ref[h, q_mod] = top
            total_ref[h, q_mod] = total
            mixed_ref[h, q_mod] = mixed

    partner_copy(VALUE).wait_recv()
    partner_copy(KEY).wait_recv()

    def first_pass(h, carry):
        attend(h, (PARTNER,), opening=True)
        return carry

    lax.fori_loop(0, heads, first_pass, 0)

    start_relay(0)
    start_relay(1)
    finish_relay(0)

    def second_pass(h, carry):
        @pl.when(h + 1 < heads)
        def _():
            start_relay(h + 2)

        finish_relay(h + 1)

        @pl.when(behind)
        def _():
            direct_copy(h).wait_recv()

        cols = pl.ds(pl.multiple_of(h * HEAD_DIM, HEAD_DIM), HEAD_DIM)
        vout[:, cols], aout[:, cols] = attend(h, (NEAR, FAR, DIRECT), closing=True)
        return carry

    lax.fori_loop(0, heads, second_pass, 0)

    for by in range(1, count_head):
        sum_copy(by).wait_send()
    for kv in (KEY, VALUE):
        partner_copy(kv).wait_send()

    @pl.when(ahead)
    def _():
        for h in range(heads):
            direct_copy(h).wait_send()
        for part in range(heads + 1):
            relay_copy(NEAR, VIDEO, part).wait_send()

    @pl.when(behind)
    def _():
        for part in range(heads + 1):
            for slot, mod in SPLIT:
                split_copy(slot, mod, part).wait_send()
            relay_copy(FAR, AUDIO, part).wait_send()


def hand_over(v_in, a_in, v_out, a_out, held, sems_in, sems_out):
    parts = held.shape[1]
    rows = held.shape[2]
    refs = ((v_in, v_out), (a_in, a_out))
    taken, given = [], []
    for i, (src, dst) in enumerate(refs):
        for p in range(parts):
            cut = pl.ds(p * rows, rows)
            taken.append(pltpu.make_async_copy(src.at[cut], held.at[i, p], sems_in.at[i, p]))
            given.append(pltpu.make_async_copy(held.at[i, p], dst.at[cut], sems_out.at[i, p]))
    for copy in taken:
        copy.start()
    for before, after in zip(taken, given):
        before.wait()
        after.start()
    for copy in given:
        copy.wait()


def local(
    video_q,
    video_k,
    video_v,
    audio_q,
    audio_k,
    audio_v,
    video_q_gain,
    audio_k_gain,
    audio_q_gain,
    video_k_gain,
    tile_first,
    tile_count,
):
    count_seq, count_head = lax.axis_size("seq"), lax.axis_size("head")
    rows, cols = video_q.shape
    heads = cols // HEAD_DIM

    def body(*refs):
        kernel(count_seq, count_head, *refs)

    hbm = pl.BlockSpec(memory_space=pl.ANY)
    vmem = pl.BlockSpec(memory_space=pltpu.VMEM)
    smem = pl.BlockSpec(memory_space=pltpu.SMEM)
    both = (jax.ShapeDtypeStruct((rows, cols), jnp.bfloat16),) * 2
    dma = pltpu.SemaphoreType.DMA
    v_out, a_out = pl.pallas_call(
        body,
        out_shape=both,
        in_specs=[hbm] * 6 + [vmem] * 4 + [smem] * 2,
        out_specs=(vmem, vmem),
        scratch_shapes=[
            pltpu.VMEM((4, rows, cols), jnp.bfloat16),
            pltpu.VMEM((heads, 2, rows, HEAD_DIM), jnp.bfloat16),
            pltpu.VMEM((heads, 2, 2, rows, HEAD_DIM), jnp.bfloat16),
            pltpu.VMEM((heads, 2, rows, HEAD_DIM), jnp.bfloat16),
            pltpu.VMEM((4, heads, 2, 2, rows, HEAD_DIM), jnp.bfloat16),
            pltpu.VMEM((heads, 2, 1, rows), jnp.float32),
            pltpu.VMEM((heads, 2, 1, rows), jnp.float32),
            pltpu.VMEM((heads, 2, HEAD_DIM, rows), jnp.float32),
            pltpu.VMEM((8, rows), jnp.float32),
            pltpu.VMEM((count_head - 1, 8, rows), jnp.float32),
            dma((4,)),
            dma((2, heads)),
            dma((count_head - 1,)),
            dma((count_head - 1,)),
            dma((2,)),
            dma((2,)),
            dma((2, heads + 1)),
            dma((2, heads + 1)),
            dma((2, heads + 1)),
            dma((2, heads + 1)),
            dma((heads,)),
            dma((heads,)),
        ],
        compiler_params=pltpu.CompilerParams(
            collective_id=0, has_side_effects=True, vmem_limit_bytes=56 * 1024 * 1024
        ),
        name="attend",
    )(
        video_q,
        video_k,
        video_v,
        audio_q,
        audio_k,
        audio_v,
        video_q_gain,
        audio_k_gain,
        audio_q_gain,
        video_k_gain,
        tile_first,
        tile_count,
    )
    return pl.pallas_call(
        hand_over,
        out_shape=both,
        in_specs=[hbm] * 2,
        out_specs=(hbm, hbm),
        scratch_shapes=[
            pltpu.VMEM((2, 2, rows // 2, cols), jnp.bfloat16),
            dma((2, 2)),
            dma((2, 2)),
        ],
        compiler_params=pltpu.CompilerParams(vmem_limit_bytes=56 * 1024 * 1024),
        name="hand_over",
    )(v_out, a_out)


def solution(mesh):
    return jax.shard_map(
        local,
        mesh=mesh,
        in_specs=(P("seq", "head"),) * 6 + (P("head"),) * 4 + (P(), P()),
        out_specs=(P("seq", "head"), P("seq", "head")),
        check_vma=False,
    )
```

time: 54.8 us -> 47.5 us (0.87)
  the two profiles are of different devices: /device:TPU:1 before, /device:TPU:121 now
where the time goes in v2:
time: 47.5 us; the launch traced here: 47.3 us
  Pallas kernels  46.7 us (98%)
  between operations  0.64 us (1%)
    pallas_call x1, Pallas kernels, local(): pl.pallas_call(body, out_shape=both, in_specs=[hbm] * 6 + [vmem] * 4 + [s...  44.7 us
    pallas_call x1, Pallas kernels, local(): pl.pallas_call(hand_over, out_shape=both, in_specs=[hbm] * 2, out_specs=(...  1.97 us

profile of v2, /device:TPU:121, one launch (start us, length us, event | category | flops | bytes accessed | tf_op | source)
XLA Modules:
  0.0 47.3 jit_solution(7208994249584947343)
XLA Ops:
  0.6 44.7 %attend.1 = (bf16[256,768]{1,0:T(8,128)(2,1)}, bf16[256,768]{1,0:T(8,128)(2,1)}) custom-call(bf16[256,768]{1,0:T(8,128)(2,1)} %refs_0_.1, bf16[256,768]{1,0:T(8,128)(2,1)} %refs_1_.1, bf16[256,768]{1,0:T(8,128)(2,1)} %refs_2_.1, bf16[256,768]{1,0:T(8,128)(2,1)} %refs_3_.1, bf16[256,768]{1,0:T(8,128)(2,1)} %refs_4_.1, bf16[256,768]{1,0:T(8,128)(2,1)} %refs_5_.1, ...), custom_call_target="tpu_custom_call" | custom-call | tf_op jit(solution)/shard_map/attend/pallas_call | solution.py:405
  45.4 2.0 %hand_over.1 = (bf16[256,768]{1,0:T(8,128)(2,1)}, bf16[256,768]{1,0:T(8,128)(2,1)}) custom-call(bf16[256,768]{1,0:T(8,128)(2,1)} %get-tuple-element.4.v_in, bf16[256,768]{1,0:T(8,128)(2,1)} %get-tuple-element.5.a_in), custom_call_target="tpu_custom_call" | custom-call | tf_op jit(solution)/shard_map/hand_over/pallas_call | solution.py:452

commit v3 on v2

--- a/solution.py
+++ b/solution.py
@@ -326,16 +326,24 @@
             start_relay(h + 2)
 
         finish_relay(h + 1)
-
+        attend(h, (NEAR, FAR))
+
+        @pl.when(h >= 1)
+        def _():
+            last_pass(h - 1)
+
+        return carry
+
+    def last_pass(h):
         @pl.when(behind)
         def _():
             direct_copy(h).wait_recv()
 
         cols = pl.ds(pl.multiple_of(h * HEAD_DIM, HEAD_DIM), HEAD_DIM)
-        vout[:, cols], aout[:, cols] = attend(h, (NEAR, FAR, DIRECT), closing=True)
-        return carry
+        vout[:, cols], aout[:, cols] = attend(h, (DIRECT,), closing=True)
 
     lax.fori_loop(0, heads, second_pass, 0)
+    last_pass(heads - 1)
 
     for by in range(1, count_head):
         sum_copy(by).wait_send()
@@ -357,22 +365,17 @@
             relay_copy(FAR, AUDIO, part).wait_send()
 
 
-def hand_over(v_in, a_in, v_out, a_out, held, sems_in, sems_out):
-    parts = held.shape[1]
-    rows = held.shape[2]
-    refs = ((v_in, v_out), (a_in, a_out))
-    taken, given = [], []
-    for i, (src, dst) in enumerate(refs):
+def hand_over(v_in, a_in, v_out, a_out, sems):
+    parts = sems.shape[1]
+    rows = v_in.shape[0] // parts
+    copies = []
+    for i, (src, dst) in enumerate(((v_in, v_out), (a_in, a_out))):
         for p in range(parts):
             cut = pl.ds(p * rows, rows)
-            taken.append(pltpu.make_async_copy(src.at[cut], held.at[i, p], sems_in.at[i, p]))
-            given.append(pltpu.make_async_copy(held.at[i, p], dst.at[cut], sems_out.at[i, p]))
-    for copy in taken:
+            copies.append(pltpu.make_async_copy(src.at[cut], dst.at[cut], sems.at[i, p]))
+    for copy in copies:
         copy.start()
-    for before, after in zip(taken, given):
-        before.wait()
-        after.start()
-    for copy in given:
+    for copy in copies:
         copy.wait()
 
 
@@ -404,7 +407,7 @@
     dma = pltpu.SemaphoreType.DMA
     v_out, a_out = pl.pallas_call(
         body,
-        out_shape=both,
+        out_shape=(pltpu.VMEM((rows, cols), jnp.bfloat16),) * 2,
         in_specs=[hbm] * 6 + [vmem] * 4 + [smem] * 2,
         out_specs=(vmem, vmem),
         scratch_shapes=[
@@ -432,36 +435,37 @@
             dma((heads,)),
         ],
         compiler_params=pltpu.CompilerParams(
-            collective_id=0, has_side_effects=True, vmem_limit_bytes=56 * 1024 * 1024
+            collective_id=0, has_side_effects=True, vmem_limit_bytes=40 * 1024 * 1024
         ),
         name="attend",
     )(
-        video_q,
-        video_k,
-        video_v,
-        audio_q,
-        audio_k,
-        audio_v,
-        video_q_gain,
-        audio_k_gain,
-        audio_q_gain,
-        video_k_gain,
-        tile_first,
-        tile_count,
+        *(
+            pltpu.with_memory_space_constraint(x, pltpu.HBM)
+            for x in (
+                video_q,
+                video_k,
+                video_v,
+                audio_q,
+                audio_k,
+                audio_v,
+                video_q_gain,
+                audio_k_gain,
+                audio_q_gain,
+                video_k_gain,
+                tile_first,
+                tile_count,
+            )
+        )
     )
     return pl.pallas_call(
         hand_over,
         out_shape=both,
-        in_specs=[hbm] * 2,
+        in_specs=[vmem] * 2,
         out_specs=(hbm, hbm),
-        scratch_shapes=[
-            pltpu.VMEM((2, 2, rows // 2, cols), jnp.bfloat16),
-            dma((2, 2)),
-            dma((2, 2)),
-        ],
-        compiler_params=pltpu.CompilerParams(vmem_limit_bytes=56 * 1024 * 1024),
+        scratch_shapes=[dma((2, 2))],
+        compiler_params=pltpu.CompilerParams(vmem_limit_bytes=4 * 1024 * 1024),
         name="hand_over",
-    )(v_out, a_out)
+    )(*(pltpu.with_memory_space_constraint(x, pltpu.VMEM) for x in (v_out, a_out)))
 
 
 def solution(mesh):

time: 47.5 us -> 45.6 us (0.960)
  Pallas kernels: 46.7 us -> 44.4 us
    pallas_call x2, Pallas kernels: 46.7 us -> 44.4 us  [the longest x1 43.5 us: local(): pl.pallas_call(body, out_shape=(pltpu.VMEM((rows, cols), jnp.bfloat16),)...]
where the time goes in v3:
time: 45.6 us; the launch traced here: 45 us
  Pallas kernels  44.4 us (97%)
  between operations  0.64 us (1%)
    pallas_call x1, Pallas kernels, local(): pl.pallas_call(body, out_shape=(pltpu.VMEM((rows, cols), jnp.bfloat16),)...  43.5 us

profile of v3, /device:TPU:121, one launch (start us, length us, event | category | flops | bytes accessed | tf_op | source)
XLA Modules:
  0.0 45.0 jit_solution(37903560138056342)
XLA Ops:
  0.6 43.5 %attend.1 = (bf16[256,768]{1,0:T(8,128)(2,1)S(1)}, bf16[256,768]{1,0:T(8,128)(2,1)S(1)}) custom-call(bf16[256,768]{1,0:T(8,128)(2,1)} %refs_0_.1, bf16[256,768]{1,0:T(8,128)(2,1)} %refs_1_.1, bf16[256,768]{1,0:T(8,128)(2,1)} %refs_2_.1, bf16[256,768]{1,0:T(8,128)(2,1)} %refs_3_.1, bf16[256,768]{1,0:T(8,128)(2,1)} %refs_4_.1, bf16[256,768]{1,0:T(8,128)(2,1)} %refs_5_.1, ...), custom_call_target="tpu_custom_call" | custom-call | tf_op jit(solution)/shard_map/attend/pallas_call | solution.py:408
  44.1 0.9 %hand_over.1 = (bf16[256,768]{1,0:T(8,128)(2,1)}, bf16[256,768]{1,0:T(8,128)(2,1)}) custom-call(bf16[256,768]{1,0:T(8,128)(2,1)S(1)} %get-tuple-element.4.v_in, bf16[256,768]{1,0:T(8,128)(2,1)S(1)} %get-tuple-element.5.a_in), custom_call_target="tpu_custom_call" | custom-call | tf_op jit(solution)/shard_map/hand_over/pallas_call | solution.py:460

commit v4 on v3

--- a/solution.py
+++ b/solution.py
@@ -8,6 +8,7 @@
 HEAD_DIM = 128
 EPS = 1e-06
 NEG = -1e30
+EARLY = 2
 MESH = pl.DeviceIdType.MESH
 LOG2E = 1.4426950408889634
 FACTOR = LOG2E * HEAD_DIM**-0.5
@@ -47,8 +48,11 @@
     mixed_ref,
     sums,
     sums_in,
+    all_sums,
     local_sem,
     value_sem,
+    pair_send,
+    pair_recv,
     sum_send,
     sum_recv,
     partner_send,
@@ -88,10 +92,15 @@
         pl.semaphore_signal(barrier, inc=1, device_id=(seq + by * sigma, head), device_id_type=MESH)
 
     greet(1)
-    for by in range(1, count_head):
-        pl.semaphore_signal(
-            barrier, inc=1, device_id=(seq, lax.rem(head + by, count_head)), device_id_type=MESH
-        )
+
+    lead = sigma > 0
+
+    @pl.when(lead)
+    def _():
+        for by in range(1, count_head):
+            pl.semaphore_signal(
+                barrier, inc=1, device_id=(seq, lax.rem(head + by, count_head)), device_id_type=MESH
+            )
 
     @pl.when(behind)
     def _():
@@ -110,7 +119,8 @@
         for mod in (AUDIO, VIDEO):
             for r in range(0, rows, HEAD_DIM):
                 own[h, mod, VALUE, r : r + HEAD_DIM] = jnp.transpose(raw_v[h, mod, r : r + HEAD_DIM])
-    peers = count_head + 2 * behind.astype(jnp.int32) + ahead.astype(jnp.int32)
+    peers = 1 + 2 * behind.astype(jnp.int32) + ahead.astype(jnp.int32)
+    peers += (count_head - 1) * lead.astype(jnp.int32)
     pl.semaphore_wait(barrier, peers)
 
     def remote(src, dst, send, recv, by):
@@ -151,8 +161,19 @@
     def partner_copy(kv):
         return remote(own.at[:, :, kv], far.at[PARTNER, :, :, kv], partner_send.at[kv], partner_recv.at[kv], 1)
 
-    def direct_copy(h):
-        return remote(own.at[h], far.at[DIRECT, h], direct_send.at[h], direct_recv.at[h], 2)
+    def direct_copy(part):
+        def block(ref):
+            if part == 0:
+                return ref.at[pl.ds(0, EARLY), :, VALUE]
+            if part == 1:
+                return ref.at[pl.ds(0, EARLY), :, KEY]
+            return ref.at[part - 2 + EARLY]
+
+        return remote(
+            block(own), block(far.at[DIRECT]), direct_send.at[part], direct_recv.at[part], 2
+        )
+
+    direct_parts = heads - EARLY + 2
 
     def start_split(part):
         @pl.when(behind)
@@ -181,6 +202,11 @@
             relay_copy(NEAR, VIDEO, part).wait_recv()
 
     start_split(0)
+
+    @pl.when(ahead)
+    def _():
+        direct_copy(0).start()
+
     partner_copy(VALUE).start()
 
     def clear(slot):
@@ -208,7 +234,8 @@
             wide = raw[i, :, h * HEAD_DIM : (h + 1) * HEAD_DIM].astype(jnp.float32)
             total += wide * wide
         packed = jnp.where(lane == i, jnp.sum(total, axis=1, keepdims=True), packed)
-    sums[...] = jnp.transpose(packed)[:8]
+    core = lax.rem(seq, 2)
+    sums[core] = jnp.transpose(packed)[:8]
 
     def sum_copy(by):
         return pltpu.make_async_remote_copy(
@@ -220,13 +247,27 @@
             device_id_type=MESH,
         )
 
-    for by in range(1, count_head):
-        sum_copy(by).start()
-    all_sums = sums[...]
-    for by in range(1, count_head):
-        sum_copy(by).wait_recv()
-        all_sums += sums_in[by - 1]
-    scale = lax.rsqrt(all_sums / width + EPS)
+    up_copy = remote(sums.at[1], sums.at[1], pair_send.at[0], pair_recv.at[0], 1)
+    back_copy = remote(all_sums.at[1], all_sums.at[1], pair_send.at[1], pair_recv.at[1], 1)
+
+    @pl.when(lead)
+    def _():
+        up_copy.wait_recv()
+        for by in range(1, count_head):
+            sum_copy(by).start()
+        total = sums[...]
+        for by in range(1, count_head):
+            sum_copy(by).wait_recv()
+            total += sums_in[by - 1]
+        all_sums[...] = total
+        back_copy.start()
+
+    @pl.when(jnp.logical_not(lead))
+    def _():
+        up_copy.start()
+        back_copy.wait_recv()
+
+    scale = lax.rsqrt(all_sums[core] / width + EPS)
     scale = jnp.transpose(jnp.concatenate([scale] * (HEAD_DIM // 8), axis=0))
 
     def normalized(i, gain, h):
@@ -238,10 +279,6 @@
         own[h, AUDIO, KEY] = normalized(0, akg, h)
         own[h, VIDEO, KEY] = normalized(1, vkg, h)
         start_split(h + 1)
-
-        @pl.when(ahead)
-        def _():
-            direct_copy(h).start()
 
     partner_copy(KEY).start()
     for h in range(heads):
@@ -315,6 +352,11 @@
         return carry
 
     lax.fori_loop(0, heads, first_pass, 0)
+    @pl.when(ahead)
+    def _():
+        for part in range(1, direct_parts):
+            direct_copy(part).start()
+
 
     start_relay(0)
     start_relay(1)
@@ -335,27 +377,35 @@
         return carry
 
     def last_pass(h):
-        @pl.when(behind)
-        def _():
-            direct_copy(h).wait_recv()
+        @pl.when(behind & (h == 0))
+        def _():
+            direct_copy(0).wait_recv()
+            direct_copy(1).wait_recv()
+
+        @pl.when(behind & (h >= EARLY))
+        def _():
+            arrived = h - EARLY + 2
+            remote(
+                own.at[h], far.at[DIRECT, h], direct_send.at[arrived], direct_recv.at[arrived], 2
+            ).wait_recv()
 
         cols = pl.ds(pl.multiple_of(h * HEAD_DIM, HEAD_DIM), HEAD_DIM)
         vout[:, cols], aout[:, cols] = attend(h, (DIRECT,), closing=True)
 
     lax.fori_loop(0, heads, second_pass, 0)
-    last_pass(heads - 1)
-
-    for by in range(1, count_head):
-        sum_copy(by).wait_send()
+
+    @pl.when(lead)
+    def _():
+        for by in range(1, count_head):
+            sum_copy(by).wait_send()
+        back_copy.wait_send()
+
+    @pl.when(jnp.logical_not(lead))
+    def _():
+        up_copy.wait_send()
+
     for kv in (KEY, VALUE):
         partner_copy(kv).wait_send()
-
-    @pl.when(ahead)
-    def _():
-        for h in range(heads):
-            direct_copy(h).wait_send()
-        for part in range(heads + 1):
-            relay_copy(NEAR, VIDEO, part).wait_send()
 
     @pl.when(behind)
     def _():
@@ -363,6 +413,19 @@
             for slot, mod in SPLIT:
                 split_copy(slot, mod, part).wait_send()
             relay_copy(FAR, AUDIO, part).wait_send()
+
+    @pl.when(ahead)
+    def _():
+        for part in range(heads + 1):
+            relay_copy(NEAR, VIDEO, part).wait_send()
+        for part in range(direct_parts - 1):
+            direct_copy(part).wait_send()
+
+    last_pass(heads - 1)
+
+    @pl.when(ahead)
+    def _():
+        direct_copy(direct_parts - 1).wait_send()
 
 
 def hand_over(v_in, a_in, v_out, a_out, sems):
@@ -419,10 +482,13 @@
             pltpu.VMEM((heads, 2, 1, rows), jnp.float32),
             pltpu.VMEM((heads, 2, 1, rows), jnp.float32),
             pltpu.VMEM((heads, 2, HEAD_DIM, rows), jnp.float32),
-            pltpu.VMEM((8, rows), jnp.float32),
-            pltpu.VMEM((count_head - 1, 8, rows), jnp.float32),
+            pltpu.VMEM((2, 8, rows), jnp.float32),
+            pltpu.VMEM((count_head - 1, 2, 8, rows), jnp.float32),
+            pltpu.VMEM((2, 8, rows), jnp.float32),
             dma((4,)),
             dma((2, heads)),
+            dma((2,)),
+            dma((2,)),
             dma((count_head - 1,)),
             dma((count_head - 1,)),
             dma((2,)),
@@ -431,8 +497,8 @@
             dma((2, heads + 1)),
             dma((2, heads + 1)),
             dma((2, heads + 1)),
-            dma((heads,)),
-            dma((heads,)),
+            dma((heads - EARLY + 2,)),
+            dma((heads - EARLY + 2,)),
         ],
         compiler_params=pltpu.CompilerParams(
             collective_id=0, has_side_effects=True, vmem_limit_bytes=40 * 1024 * 1024
@@ -462,7 +528,7 @@
         out_shape=both,
         in_specs=[vmem] * 2,
         out_specs=(hbm, hbm),
-        scratch_shapes=[dma((2, 2))],
+        scratch_shapes=[dma((2, 1))],
         compiler_params=pltpu.CompilerParams(vmem_limit_bytes=4 * 1024 * 1024),
         name="hand_over",
     )(*(pltpu.with_memory_space_constraint(x, pltpu.VMEM) for x in (v_out, a_out)))

time: 45.6 us -> 44.1 us (0.967)
  Pallas kernels: 44.4 us -> 42.8 us
    pallas_call x1, Pallas kernels: 43.5 us -> 41.9 us  [local(): pl.pallas_call(body, out_shape=(pltpu.VMEM((rows, cols), jnp.bfloat16),)...]
where the time goes in v4:
time: 44.1 us; the launch traced here: 43.4 us
  Pallas kernels  42.8 us (97%)
  between operations  0.64 us (1%)
    pallas_call x1, Pallas kernels, local(): pl.pallas_call(body, out_shape=(pltpu.VMEM((rows, cols), jnp.bfloat16),)...  41.9 us
    pallas_call x1, Pallas kernels, local(): pl.pallas_call(hand_over, out_shape=both, in_specs=[vmem] * 2, out_specs=...  0.89 us

profile of v4, /device:TPU:121, one launch (start us, length us, event | category | flops | bytes accessed | tf_op | source)
XLA Modules:
  0.0 43.4 jit_solution(5908591697099911546)
XLA Ops:
  0.6 41.9 %attend.1 = (bf16[256,768]{1,0:T(8,128)(2,1)S(1)}, bf16[256,768]{1,0:T(8,128)(2,1)S(1)}) custom-call(bf16[256,768]{1,0:T(8,128)(2,1)} %refs_0_.1, bf16[256,768]{1,0:T(8,128)(2,1)} %refs_1_.1, bf16[256,768]{1,0:T(8,128)(2,1)} %refs_2_.1, bf16[256,768]{1,0:T(8,128)(2,1)} %refs_3_.1, bf16[256,768]{1,0:T(8,128)(2,1)} %refs_4_.1, bf16[256,768]{1,0:T(8,128)(2,1)} %refs_5_.1, ...), custom_call_target="tpu_custom_call" | custom-call | tf_op jit(solution)/shard_map/attend/pallas_call | solution.py:471
  42.5 0.9 %hand_over.1 = (bf16[256,768]{1,0:T(8,128)(2,1)}, bf16[256,768]{1,0:T(8,128)(2,1)}) custom-call(bf16[256,768]{1,0:T(8,128)(2,1)S(1)} %get-tuple-element.4.v_in, bf16[256,768]{1,0:T(8,128)(2,1)S(1)} %get-tuple-element.5.a_in), custom_call_target="tpu_custom_call" | custom-call | tf_op jit(solution)/shard_map/hand_over/pallas_call | solution.py:526

commit v5 on v4

--- a/solution.py
+++ b/solution.py
@@ -30,14 +30,21 @@
     aq_hbm,
     ak_hbm,
     av_hbm,
+    vqg_hbm,
+    akg_hbm,
+    aqg_hbm,
+    vkg_hbm,
+    first_hbm,
+    count_hbm,
+    vout,
+    aout,
     vqg,
     akg,
     aqg,
     vkg,
     first_ref,
     count_ref,
-    vout,
-    aout,
+    small_sem,
     raw,
     raw_v,
     own,
@@ -86,10 +93,32 @@
                     value_sem.at[mod, h],
                 )
             )
+    smalls = [
+        pltpu.make_async_copy(src, dst, small_sem.at[i])
+        for i, (src, dst) in enumerate(
+            (
+                (akg_hbm, akg),
+                (vkg_hbm, vkg),
+                (vqg_hbm, vqg),
+                (aqg_hbm, aqg),
+                (first_hbm, first_ref),
+                (count_hbm, count_ref),
+            )
+        )
+    ]
     barrier = pltpu.get_barrier_semaphore()
 
     def greet(by):
         pl.semaphore_signal(barrier, inc=1, device_id=(seq + by * sigma, head), device_id_type=MESH)
+
+    @pl.when(behind)
+    def _():
+        greet(-1)
+        greet(-2)
+
+    @pl.when(ahead)
+    def _():
+        greet(2)
 
     greet(1)
 
@@ -102,16 +131,7 @@
                 barrier, inc=1, device_id=(seq, lax.rem(head + by, count_head)), device_id_type=MESH
             )
 
-    @pl.when(behind)
-    def _():
-        greet(-1)
-        greet(-2)
-
-    @pl.when(ahead)
-    def _():
-        greet(2)
-
-    for load in value_loads + loads:
+    for load in value_loads + loads + smalls:
         load.start()
     for load in value_loads:
         load.wait()
@@ -167,13 +187,17 @@
                 return ref.at[pl.ds(0, EARLY), :, VALUE]
             if part == 1:
                 return ref.at[pl.ds(0, EARLY), :, KEY]
+            if part == direct_parts - 3:
+                return ref.at[heads - 1, :, KEY]
+            if part >= direct_parts - 2:
+                return ref.at[heads - 1, part - direct_parts + 2, VALUE]
             return ref.at[part - 2 + EARLY]
 
         return remote(
             block(own), block(far.at[DIRECT]), direct_send.at[part], direct_recv.at[part], 2
         )
 
-    direct_parts = heads - EARLY + 2
+    direct_parts = heads - EARLY + 4
 
     def start_split(part):
         @pl.when(behind)
@@ -234,6 +258,8 @@
             wide = raw[i, :, h * HEAD_DIM : (h + 1) * HEAD_DIM].astype(jnp.float32)
             total += wide * wide
         packed = jnp.where(lane == i, jnp.sum(total, axis=1, keepdims=True), packed)
+    for load in smalls:
+        load.wait()
     core = lax.rem(seq, 2)
     sums[core] = jnp.transpose(packed)[:8]
 
@@ -297,7 +323,7 @@
         bias[VIDEO].append(jnp.where(covers(other, seq), 0.0, NEG))
         bias[AUDIO].append(jnp.where(covers(seq, other), 0.0, NEG))
 
-    def attend(h, slots, opening=False, closing=False):
+    def attend(h, slots, opening=False, closing=False, ready=None):
         jobs = []
         for q_mod in (VIDEO, AUDIO):
             refs = [(far.at[slot, h, 1 - q_mod], bias[q_mod][slot]) for slot in slots]
@@ -318,31 +344,37 @@
                 most = jnp.max(score, axis=0, keepdims=True) + add
                 top = most if top is None else jnp.maximum(top, most)
             tops.append(top)
-        results = []
+        parts = []
         for (q_mod, refs, scores), top in zip(jobs, tops):
-            total, mixed = None, None
-            for score, (ref, add) in zip(scores, refs):
-                weights = jnp.exp2((score - (top - add)) * FACTOR)
-                part = jnp.sum(weights, axis=0, keepdims=True)
+            total, weights = None, []
+            for score, (_, add) in zip(scores, refs):
+                weight = jnp.exp2((score - (top - add)) * FACTOR)
+                part = jnp.sum(weight, axis=0, keepdims=True)
+                total = part if total is None else total + part
+                weights.append(weight.astype(jnp.bfloat16))
+            fade = None
+            if not opening:
+                fade = jnp.exp2((top_ref[h, q_mod] - top) * FACTOR)
+                total += total_ref[h, q_mod] * fade
+            parts.append((q_mod, refs, top, total, weights, fade))
+        for q_mod, refs, top, total, weights, fade in parts:
+            if ready is not None:
+                ready(1 - q_mod)
+            mixed = None if opening else mixed_ref[h, q_mod] * fade
+            for weight, (ref, _) in zip(weights, refs):
                 value = jnp.concatenate(
                     [ref[VALUE, r : r + HEAD_DIM] for r in range(0, rows, HEAD_DIM)], axis=1
                 )
-                block = jnp.dot(
-                    value, weights.astype(jnp.bfloat16), preferred_element_type=jnp.float32
-                )
-                total = part if total is None else total + part
+                block = jnp.dot(value, weight, preferred_element_type=jnp.float32)
                 mixed = block if mixed is None else mixed + block
-            if not opening:
-                fade = jnp.exp2((top_ref[h, q_mod] - top) * FACTOR)
-                total += total_ref[h, q_mod] * fade
-                mixed += mixed_ref[h, q_mod] * fade
-            results.append((q_mod, top, total, mixed))
-        if closing:
-            return [jnp.transpose(mixed / total).astype(jnp.bfloat16) for _, _, total, mixed in results]
-        for q_mod, top, total, mixed in results:
-            top_ref[h, q_mod] = top
-            total_ref[h, q_mod] = total
-            mixed_ref[h, q_mod] = mixed
+            if closing:
+                cols = pl.ds(pl.multiple_of(h * HEAD_DIM, HEAD_DIM), HEAD_DIM)
+                out = vout if q_mod == VIDEO else aout
+                out[:, cols] = jnp.transpose(mixed / total).astype(jnp.bfloat16)
+            else:
+                top_ref[h, q_mod] = top
+                total_ref[h, q_mod] = total
+                mixed_ref[h, q_mod] = mixed
 
     partner_copy(VALUE).wait_recv()
     partner_copy(KEY).wait_recv()
@@ -389,8 +421,12 @@
                 own.at[h], far.at[DIRECT, h], direct_send.at[arrived], direct_recv.at[arrived], 2
             ).wait_recv()
 
-        cols = pl.ds(pl.multiple_of(h * HEAD_DIM, HEAD_DIM), HEAD_DIM)
-        vout[:, cols], aout[:, cols] = attend(h, (DIRECT,), closing=True)
+        attend(h, (DIRECT,), closing=True)
+
+    def arrive(part):
+        @pl.when(behind)
+        def _():
+            direct_copy(part).wait_recv()
 
     lax.fori_loop(0, heads, second_pass, 0)
 
@@ -421,7 +457,13 @@
         for part in range(direct_parts - 1):
             direct_copy(part).wait_send()
 
-    last_pass(heads - 1)
+    arrive(direct_parts - 3)
+    attend(
+        heads - 1,
+        (DIRECT,),
+        closing=True,
+        ready=lambda mod: arrive(direct_parts - 2 + mod),
+    )
 
     @pl.when(ahead)
     def _():
@@ -465,15 +507,17 @@
 
     hbm = pl.BlockSpec(memory_space=pl.ANY)
     vmem = pl.BlockSpec(memory_space=pltpu.VMEM)
-    smem = pl.BlockSpec(memory_space=pltpu.SMEM)
     both = (jax.ShapeDtypeStruct((rows, cols), jnp.bfloat16),) * 2
     dma = pltpu.SemaphoreType.DMA
     v_out, a_out = pl.pallas_call(
         body,
         out_shape=(pltpu.VMEM((rows, cols), jnp.bfloat16),) * 2,
-        in_specs=[hbm] * 6 + [vmem] * 4 + [smem] * 2,
+        in_specs=[hbm] * 12,
         out_specs=(vmem, vmem),
         scratch_shapes=[
+            *[pltpu.VMEM((cols,), jnp.float32)] * 4,
+            *[pltpu.SMEM((count_seq,), jnp.int32)] * 2,
+            dma((6,)),
             pltpu.VMEM((4, rows, cols), jnp.bfloat16),
             pltpu.VMEM((heads, 2, rows, HEAD_DIM), jnp.bfloat16),
             pltpu.VMEM((heads, 2, 2, rows, HEAD_DIM), jnp.bfloat16),
@@ -497,8 +541,8 @@
             dma((2, heads + 1)),
             dma((2, heads + 1)),
             dma((2, heads + 1)),
-            dma((heads - EARLY + 2,)),
-            dma((heads - EARLY + 2,)),
+            dma((heads - EARLY + 4,)),
+            dma((heads - EARLY + 4,)),
         ],
         compiler_params=pltpu.CompilerParams(
             collective_id=0, has_side_effects=True, vmem_limit_bytes=40 * 1024 * 1024

time: 44.1 us -> 43 us (0.975)
  Pallas kernels: 42.8 us -> 41.8 us
    pallas_call x1, Pallas kernels: 41.9 us -> 40.9 us  [local(): pl.pallas_call(body, out_shape=(pltpu.VMEM((rows, cols), jnp.bfloat16),)...]
where the time goes in v5:
time: 43 us; the launch traced here: 42.4 us
  Pallas kernels  41.8 us (97%)
  between operations  0.64 us (1%)
    pallas_call x1, Pallas kernels, local(): pl.pallas_call(body, out_shape=(pltpu.VMEM((rows, cols), jnp.bfloat16),)...  40.9 us
    pallas_call x1, Pallas kernels, local(): pl.pallas_call(hand_over, out_shape=both, in_specs=[vmem] * 2, out_specs=...  0.89 us

profile of v5, /device:TPU:121, one launch (start us, length us, event | category | flops | bytes accessed | tf_op | source)
XLA Modules:
  0.0 42.4 jit_solution(7479330197314612634)
XLA Ops:
  0.6 40.9 %attend.1 = (bf16[256,768]{1,0:T(8,128)(2,1)S(1)}, bf16[256,768]{1,0:T(8,128)(2,1)S(1)}) custom-call(bf16[256,768]{1,0:T(8,128)(2,1)} %refs_0_.1, bf16[256,768]{1,0:T(8,128)(2,1)} %refs_1_.1, bf16[256,768]{1,0:T(8,128)(2,1)} %refs_2_.1, bf16[256,768]{1,0:T(8,128)(2,1)} %refs_3_.1, bf16[256,768]{1,0:T(8,128)(2,1)} %refs_4_.1, bf16[256,768]{1,0:T(8,128)(2,1)} %refs_5_.1, ...), custom_call_target="tpu_custom_call" | custom-call | tf_op jit(solution)/shard_map/attend/pallas_call | solution.py:512
  41.5 0.9 %hand_over.1 = (bf16[256,768]{1,0:T(8,128)(2,1)}, bf16[256,768]{1,0:T(8,128)(2,1)}) custom-call(bf16[256,768]{1,0:T(8,128)(2,1)S(1)} %get-tuple-element.4.v_in, bf16[256,768]{1,0:T(8,128)(2,1)S(1)} %get-tuple-element.5.a_in), custom_call_target="tpu_custom_call" | custom-call | tf_op jit(solution)/shard_map/hand_over/pallas_call | solution.py:570

commit v6 on v5

--- a/solution.py
+++ b/solution.py
@@ -83,16 +83,10 @@
     loads = []
     for i, ref in enumerate((ak_hbm, vk_hbm, vq_hbm, aq_hbm)):
         loads.append(pltpu.make_async_copy(ref, raw.at[i], local_sem.at[i]))
-    value_loads = []
-    for mod, ref in enumerate((av_hbm, vv_hbm)):
-        for h in range(heads):
-            value_loads.append(
-                pltpu.make_async_copy(
-                    ref.at[:, pl.ds(h * HEAD_DIM, HEAD_DIM)],
-                    raw_v.at[h, mod],
-                    value_sem.at[mod, h],
-                )
-            )
+    value_loads = [
+        pltpu.make_async_copy(ref, raw_v.at[mod], value_sem.at[mod])
+        for mod, ref in enumerate((av_hbm, vv_hbm))
+    ]
     smalls = [
         pltpu.make_async_copy(src, dst, small_sem.at[i])
         for i, (src, dst) in enumerate(
@@ -131,14 +125,16 @@
                 barrier, inc=1, device_id=(seq, lax.rem(head + by, count_head)), device_id_type=MESH
             )
 
-    for load in value_loads + loads + smalls:
+    for load in value_loads:
         load.start()
     for load in value_loads:
         load.wait()
     for h in range(heads):
         for mod in (AUDIO, VIDEO):
             for r in range(0, rows, HEAD_DIM):
-                own[h, mod, VALUE, r : r + HEAD_DIM] = jnp.transpose(raw_v[h, mod, r : r + HEAD_DIM])
+                own[h, mod, VALUE, r : r + HEAD_DIM] = jnp.transpose(
+                    raw_v[mod, r : r + HEAD_DIM, h * HEAD_DIM : (h + 1) * HEAD_DIM]
+                )
     peers = 1 + 2 * behind.astype(jnp.int32) + ahead.astype(jnp.int32)
     peers += (count_head - 1) * lead.astype(jnp.int32)
     pl.semaphore_wait(barrier, peers)
@@ -232,6 +228,8 @@
         direct_copy(0).start()
 
     partner_copy(VALUE).start()
+    for load in loads + smalls:
+        load.start()
 
     def clear(slot):
         def body(h, carry):
@@ -384,13 +382,13 @@
         return carry
 
     lax.fori_loop(0, heads, first_pass, 0)
+
+    start_relay(0)
     @pl.when(ahead)
     def _():
         for part in range(1, direct_parts):
             direct_copy(part).start()
 
-
-    start_relay(0)
     start_relay(1)
     finish_relay(0)
 
@@ -519,7 +517,7 @@
             *[pltpu.SMEM((count_seq,), jnp.int32)] * 2,
             dma((6,)),
             pltpu.VMEM((4, rows, cols), jnp.bfloat16),
-            pltpu.VMEM((heads, 2, rows, HEAD_DIM), jnp.bfloat16),
+            pltpu.VMEM((2, rows, cols), jnp.bfloat16),
             pltpu.VMEM((heads, 2, 2, rows, HEAD_DIM), jnp.bfloat16),
             pltpu.VMEM((heads, 2, rows, HEAD_DIM), jnp.bfloat16),
             pltpu.VMEM((4, heads, 2, 2, rows, HEAD_DIM), jnp.bfloat16),
@@ -530,7 +528,7 @@
             pltpu.VMEM((count_head - 1, 2, 8, rows), jnp.float32),
             pltpu.VMEM((2, 8, rows), jnp.float32),
             dma((4,)),
-            dma((2, heads)),
+            dma((2,)),
             dma((2,)),
             dma((2,)),
             dma((count_head - 1,)),

time: 43 us -> 43 us (level)
  no operation moved by 1% of the time
where the time goes in v6:
time: 43 us; the launch traced here: 42.3 us
  Pallas kernels  41.7 us (97%)
  between operations  0.64 us (1%)
    pallas_call x1, Pallas kernels, local(): pl.pallas_call(body, out_shape=(pltpu.VMEM((rows, cols), jnp.bfloat16),)...  40.8 us
    pallas_call x1, Pallas kernels, local(): pl.pallas_call(hand_over, out_shape=both, in_specs=[vmem] * 2, out_specs=...  0.89 us

profile of v6, /device:TPU:121, one launch (start us, length us, event | category | flops | bytes accessed | tf_op | source)
XLA Modules:
  0.0 42.3 jit_solution(15227015767894812718)
XLA Ops:
  0.6 40.8 %attend.1 = (bf16[256,768]{1,0:T(8,128)(2,1)S(1)}, bf16[256,768]{1,0:T(8,128)(2,1)S(1)}) custom-call(bf16[256,768]{1,0:T(8,128)(2,1)} %refs_0_.1, bf16[256,768]{1,0:T(8,128)(2,1)} %refs_1_.1, bf16[256,768]{1,0:T(8,128)(2,1)} %refs_2_.1, bf16[256,768]{1,0:T(8,128)(2,1)} %refs_3_.1, bf16[256,768]{1,0:T(8,128)(2,1)} %refs_4_.1, bf16[256,768]{1,0:T(8,128)(2,1)} %refs_5_.1, ...), custom_call_target="tpu_custom_call" | custom-call | tf_op jit(solution)/shard_map/attend/pallas_call | solution.py:510
  41.4 0.9 %hand_over.1 = (bf16[256,768]{1,0:T(8,128)(2,1)}, bf16[256,768]{1,0:T(8,128)(2,1)}) custom-call(bf16[256,768]{1,0:T(8,128)(2,1)S(1)} %get-tuple-element.4.v_in, bf16[256,768]{1,0:T(8,128)(2,1)S(1)} %get-tuple-element.5.a_in), custom_call_target="tpu_custom_call" | custom-call | tf_op jit(solution)/shard_map/hand_over/pallas_call | solution.py:568

commit v7 on v6

--- a/solution.py
+++ b/solution.py
@@ -9,6 +9,7 @@
 EPS = 1e-06
 NEG = -1e30
 EARLY = 2
+GROUP = 3
 MESH = pl.DeviceIdType.MESH
 LOG2E = 1.4426950408889634
 FACTOR = LOG2E * HEAD_DIM**-0.5
@@ -152,7 +153,7 @@
     def block(ref, mod, part):
         if isinstance(part, int) and part == 0:
             return ref.at[:, mod, VALUE]
-        return ref.at[part - 1, mod, KEY]
+        return ref.at[pl.ds((part - 1) * GROUP, GROUP), mod, KEY]
 
     def split_copy(slot, mod, part):
         by = -1 if slot == NEAR else -2
@@ -302,7 +303,8 @@
     for h in range(heads):
         own[h, AUDIO, KEY] = normalized(0, akg, h)
         own[h, VIDEO, KEY] = normalized(1, vkg, h)
-        start_split(h + 1)
+        if h % GROUP == GROUP - 1:
+            start_split(h // GROUP + 1)
 
     partner_copy(KEY).start()
     for h in range(heads):
@@ -393,11 +395,16 @@
     finish_relay(0)
 
     def second_pass(h, carry):
-        @pl.when(h + 1 < heads)
-        def _():
-            start_relay(h + 2)
-
-        finish_relay(h + 1)
+        part = h // GROUP + 1
+
+        @pl.when((lax.rem(h, GROUP) == 0) & (h + GROUP < heads))
+        def _():
+            start_relay(part + 1)
+
+        @pl.when(lax.rem(h, GROUP) == 0)
+        def _():
+            finish_relay(part)
+
         attend(h, (NEAR, FAR))
 
         @pl.when(h >= 1)
@@ -443,14 +450,14 @@
 
     @pl.when(behind)
     def _():
-        for part in range(heads + 1):
+        for part in range(heads // GROUP + 1):
             for slot, mod in SPLIT:
                 split_copy(slot, mod, part).wait_send()
             relay_copy(FAR, AUDIO, part).wait_send()
 
     @pl.when(ahead)
     def _():
-        for part in range(heads + 1):
+        for part in range(heads // GROUP + 1):
             relay_copy(NEAR, VIDEO, part).wait_send()
         for part in range(direct_parts - 1):
             direct_copy(part).wait_send()
@@ -535,10 +542,10 @@
             dma((count_head - 1,)),
             dma((2,)),
             dma((2,)),
-            dma((2, heads + 1)),
-            dma((2, heads + 1)),
-            dma((2, heads + 1)),
-            dma((2, heads + 1)),
+            dma((2, heads // GROUP + 1)),
+            dma((2, heads // GROUP + 1)),
+            dma((2, heads // GROUP + 1)),
+            dma((2, heads // GROUP + 1)),
             dma((heads - EARLY + 4,)),
             dma((heads - EARLY + 4,)),
         ],

time: 43 us -> 42.7 us (level)
  no operation moved by 1% of the time
where the time goes in v7:
time: 42.7 us; the launch traced here: 42 us
  Pallas kernels  41.4 us (97%)
  between operations  0.64 us (1%)
    pallas_call x1, Pallas kernels, local(): pl.pallas_call(body, out_shape=(pltpu.VMEM((rows, cols), jnp.bfloat16),)...  40.5 us
    pallas_call x1, Pallas kernels, local(): pl.pallas_call(hand_over, out_shape=both, in_specs=[vmem] * 2, out_specs=...  0.89 us

profile of v7, /device:TPU:121, one launch (start us, length us, event | category | flops | bytes accessed | tf_op | source)
XLA Modules:
  0.0 42.0 jit_solution(1928132539036387845)
XLA Ops:
  0.6 40.5 %attend.1 = (bf16[256,768]{1,0:T(8,128)(2,1)S(1)}, bf16[256,768]{1,0:T(8,128)(2,1)S(1)}) custom-call(bf16[256,768]{1,0:T(8,128)(2,1)} %refs_0_.1, bf16[256,768]{1,0:T(8,128)(2,1)} %refs_1_.1, bf16[256,768]{1,0:T(8,128)(2,1)} %refs_2_.1, bf16[256,768]{1,0:T(8,128)(2,1)} %refs_3_.1, bf16[256,768]{1,0:T(8,128)(2,1)} %refs_4_.1, bf16[256,768]{1,0:T(8,128)(2,1)} %refs_5_.1, ...), custom_call_target="tpu_custom_call" | custom-call | tf_op jit(solution)/shard_map/attend/pallas_call | solution.py:517
  41.1 0.9 %hand_over.1 = (bf16[256,768]{1,0:T(8,128)(2,1)}, bf16[256,768]{1,0:T(8,128)(2,1)}) custom-call(bf16[256,768]{1,0:T(8,128)(2,1)S(1)} %get-tuple-element.4.v_in, bf16[256,768]{1,0:T(8,128)(2,1)S(1)} %get-tuple-element.5.a_in), custom_call_target="tpu_custom_call" | custom-call | tf_op jit(solution)/shard_map/hand_over/pallas_call | solution.py:575

commit v8 on v7

--- a/solution.py
+++ b/solution.py
@@ -356,21 +356,27 @@
             if not opening:
                 fade = jnp.exp2((top_ref[h, q_mod] - top) * FACTOR)
                 total += total_ref[h, q_mod] * fade
-            parts.append((q_mod, refs, top, total, weights, fade))
-        for q_mod, refs, top, total, weights, fade in parts:
+            mixed = None if opening else mixed_ref[h, q_mod] * fade
+            share = None
+            if closing:
+                share = 1.0 / total
+                mixed *= share
+            parts.append((q_mod, refs, top, total, weights, mixed, share))
+        for q_mod, refs, top, total, weights, mixed, share in parts:
             if ready is not None:
                 ready(1 - q_mod)
-            mixed = None if opening else mixed_ref[h, q_mod] * fade
             for weight, (ref, _) in zip(weights, refs):
                 value = jnp.concatenate(
                     [ref[VALUE, r : r + HEAD_DIM] for r in range(0, rows, HEAD_DIM)], axis=1
                 )
                 block = jnp.dot(value, weight, preferred_element_type=jnp.float32)
+                if closing:
+                    block *= share
                 mixed = block if mixed is None else mixed + block
             if closing:
                 cols = pl.ds(pl.multiple_of(h * HEAD_DIM, HEAD_DIM), HEAD_DIM)
                 out = vout if q_mod == VIDEO else aout
-                out[:, cols] = jnp.transpose(mixed / total).astype(jnp.bfloat16)
+                out[:, cols] = jnp.transpose(mixed.astype(jnp.bfloat16))
             else:
                 top_ref[h, q_mod] = top
                 total_ref[h, q_mod] = total

time: 42.7 us -> 42.7 us (level)
  no operation moved by 1% of the time
where the time goes in v8:
time: 42.7 us; the launch traced here: 42 us
  Pallas kernels  41.4 us (97%)
  between operations  0.64 us (1%)
    pallas_call x1, Pallas kernels, local(): pl.pallas_call(body, out_shape=(pltpu.VMEM((rows, cols), jnp.bfloat16),)...  40.5 us
    pallas_call x1, Pallas kernels, local(): pl.pallas_call(hand_over, out_shape=both, in_specs=[vmem] * 2, out_specs=...  0.89 us

profile of v8, /device:TPU:121, one launch (start us, length us, event | category | flops | bytes accessed | tf_op | source)
XLA Modules:
  0.0 42.0 jit_solution(12021435043512155257)
XLA Ops:
  0.6 40.5 %attend.1 = (bf16[256,768]{1,0:T(8,128)(2,1)S(1)}, bf16[256,768]{1,0:T(8,128)(2,1)S(1)}) custom-call(bf16[256,768]{1,0:T(8,128)(2,1)} %refs_0_.1, bf16[256,768]{1,0:T(8,128)(2,1)} %refs_1_.1, bf16[256,768]{1,0:T(8,128)(2,1)} %refs_2_.1, bf16[256,768]{1,0:T(8,128)(2,1)} %refs_3_.1, bf16[256,768]{1,0:T(8,128)(2,1)} %refs_4_.1, bf16[256,768]{1,0:T(8,128)(2,1)} %refs_5_.1, ...), custom_call_target="tpu_custom_call" | custom-call | tf_op jit(solution)/shard_map/attend/pallas_call | solution.py:523
  41.1 0.9 %hand_over.1 = (bf16[256,768]{1,0:T(8,128)(2,1)}, bf16[256,768]{1,0:T(8,128)(2,1)}) custom-call(bf16[256,768]{1,0:T(8,128)(2,1)S(1)} %get-tuple-element.4.v_in, bf16[256,768]{1,0:T(8,128)(2,1)S(1)} %get-tuple-element.5.a_in), custom_call_target="tpu_custom_call" | custom-call | tf_op jit(solution)/shard_map/hand_over/pallas_call | solution.py:581
